TPU v7x, 256 devices: a whole 4x4x8 slice. The times are simulated.
256 devices in a mesh: loop: 32 (over z, y_lo, core), rep: 8 (over x, y_hi).
Axes of the slice: x: 4, y: 4 (y_hi: 2, y_lo: 2; y = y_hi * 2 + y_lo), z: 8, core: 2. Of those that a mesh axis runs over, the one named last changes fastest.
Arguments:
- node_features: bfloat16 [32768, 602], P('loop'), may hold values from -6 to 6
- weight: bfloat16 [602, 256], replicated, may hold values from -0.25 to 0.25
- degree: int32 [32768], P('loop'), may hold values from 4 to 47
- tile_index: int32 [32, 32, 32], P('loop', 'rep'), may hold values from 0 to 63, as said below
- edge_codes: int32 [32, 32, 32, 128], P('loop', 'rep'), may hold values from -1 to 16383, as said below
- cotangent: bfloat16 [32768, 256], P(('loop', 'rep')), may hold values from -6 to 6
Outputs:
- output: bfloat16 [32768, 256], P(('loop', 'rep'))
- grad_weight: float32 [602, 256], replicated
- grad_input: bfloat16 [32768, 602], P(('loop', 'rep'))
Inputs may be any that keep to these rules, and one draw needn't show every extreme that they name: `tile_index`: in each pair of owner blocks, slot r * 4 + m lies in row tile r, and the 4 slots of one row tile name distinct column tiles. `edge_codes`: codes of one tile may repeat; the share of empty slots is set per owner and can differ between owners.
All inputs are finite; a program needn't handle non-finite values.
Results may differ from a plain program's by a relative error of at most 0.007.
Values may be sent and summed in bfloat16 or wider, within the bound.
A program may use at most 64 MiB of HBM per device.

v0:
```python
import math

import jax
import jax.numpy as jnp
from jax import lax
from jax.sharding import PartitionSpec as P

TILE = 128
ROW_TILES = 8
SLOTS_ROW = 4


def shifted_2(block, axis, distance):
    devices = range(lax.axis_size(axis))
    route = [((i - distance) % len(devices), i) for i in devices]
    return lax.ppermute(block, axis, route)


def build_tiles(code_row):
    present = code_row >= 0
    clipped = jnp.maximum(code_row, 0)
    positions = lax.broadcasted_iota(jnp.int32, (1, 1, TILE), 2)
    row_onehot = (((clipped // TILE)[:, :, None] == positions) & present[:, :, None]).astype(
        jnp.bfloat16
    )
    col_onehot = ((clipped % TILE)[:, :, None] == positions).astype(jnp.bfloat16)
    counts = jnp.einsum("sea,seb->sab", row_onehot, col_onehot, preferred_element_type=jnp.float32)
    return counts.astype(jnp.bfloat16)


def forward_tiles(source, index_row, code_row):
    tile_stack = build_tiles(code_row)
    width = source.shape[1]
    pieces = source.reshape(ROW_TILES, TILE, width)[index_row % ROW_TILES]
    products = jnp.einsum("sab,sbh->sah", tile_stack, pieces, preferred_element_type=jnp.float32)
    spread = products.reshape(ROW_TILES, SLOTS_ROW, TILE, width).sum(axis=1)
    return spread.reshape(ROW_TILES * TILE, width)


def backward_tiles(source, index_row, code_row):
    tile_stack = build_tiles(code_row)
    width = source.shape[1]
    pieces = source.reshape(ROW_TILES, TILE, width)[index_row // ROW_TILES]
    products = jnp.einsum("sab,sah->sbh", tile_stack, pieces, preferred_element_type=jnp.float32)
    spread = jax.ops.segment_sum(products, index_row % ROW_TILES, num_segments=ROW_TILES)
    return spread.reshape(ROW_TILES * TILE, width)


def reduce_rows(running, share_rows):
    summed = lax.psum(running, "rep")
    return lax.dynamic_slice_in_dim(summed, lax.axis_index("rep") * share_rows, share_rows, 0)


def per_device(node_features, weight, degree, tile_index, edge_codes, cotangent):
    owner_rows = node_features.shape[0]
    hidden_width = weight.shape[1]
    loop_count = lax.axis_size("loop")
    rep_count = lax.axis_size("rep")
    steps_count = loop_count // rep_count
    levels = rep_count.bit_length() - 1
    share_rows = owner_rows // rep_count
    rep_index = lax.axis_index("rep")
    start = rep_index * share_rows
    local_index = tile_index[0]
    local_codes = edge_codes[0]
    inv_root = lax.rsqrt(degree.astype(jnp.float32))[:, None]
    proj = jnp.dot(node_features, weight, preferred_element_type=jnp.float32)
    scaled = (inv_root * proj).astype(jnp.bfloat16)
    travelling = scaled
    for level in range(levels):
        shifted = shifted_2(travelling, "loop", steps_count << level)
        travelling = jnp.where((rep_index >> level) % 2 == 1, shifted, travelling)
    running = jnp.zeros((owner_rows, hidden_width), jnp.float32)
    for position in range(steps_count):
        if position > 0:
            travelling = shifted_2(travelling, "loop", 1)
        running = running + forward_tiles(travelling, local_index[position], local_codes[position])
    own_rows = reduce_rows(running, share_rows)
    own_scaled = lax.dynamic_slice_in_dim(scaled, start, share_rows, 0).astype(jnp.float32)
    own_root = lax.dynamic_slice_in_dim(inv_root, start, share_rows, 0)
    output = (own_root * (own_rows + own_scaled)).astype(jnp.bfloat16)
    upstream_share = (own_root * cotangent.astype(jnp.float32)).astype(jnp.bfloat16)
    upstream = lax.all_gather(upstream_share, "rep", axis=0, tiled=True)
    running = backward_tiles(upstream, local_index[steps_count - 1], local_codes[steps_count - 1])
    for position in range(steps_count - 2, -1, -1):
        running = shifted_2(running, "loop", -1)
        running = running + backward_tiles(upstream, local_index[position], local_codes[position])
    for level in range(levels):
        shifted = shifted_2(running, "loop", -(steps_count << level))
        running = jnp.where((rep_index >> level) % 2 == 1, shifted, running)
    own_back = reduce_rows(running, share_rows)
    node_grad = (own_root * (own_back + upstream_share.astype(jnp.float32))).astype(jnp.bfloat16)
    own_features = lax.dynamic_slice_in_dim(node_features, start, share_rows, 0)
    partial_weight = lax.dot_general(
        own_features, node_grad, (((0,), (0,)), ((), ())), preferred_element_type=jnp.float32
    )
    total_scale = 1.0 / math.sqrt(owner_rows * loop_count)
    grad_weight = lax.psum(partial_weight, ("loop", "rep")) * total_scale
    grad_input = lax.dot_general(
        node_grad, weight, (((1,), (1,)), ((), ())), preferred_element_type=jnp.float32
    ).astype(jnp.bfloat16)
    return (output, grad_weight, grad_input)


def solution(mesh):
    return jax.shard_map(
        per_device,
        mesh=mesh,
        in_specs=(
            P("loop", None),
            P(),
            P("loop"),
            P("loop", "rep", None),
            P("loop", "rep", None, None),
            P(("loop", "rep"), None),
        ),
        out_specs=(P(("loop", "rep"), None), P(), P(("loop", "rep"), None)),
        check_vma=False,
    )
```

profile of v0, /device:TPU:1, one launch (start us, length us, event | category | flops | bytes accessed | tf_op | source)
XLA Modules:
  0.0 654.9 jit_solution(1470600016243576498)
XLA Ops:
  10.6 30.0 %all_gather.3 = bf16[1024,256]{1,0:T(8,128)(2,1)S(1)} all-gather(bf16[128,256]{1,0:T(8,128)(2,1)S(1)} %multiply_convert_fusion.1), channel_id=1, replica_groups=mesh['loop'=32,'rep'=8] {'rep'}, dimensions={0}, use_global_device_ids=true | all-gather | bytes 589824 | tf_op jit(solution)/shard_map/all_gather | solution.py:83
  41.5 2.0 gather_fusion.4
  45.1 2.7 fusion.64
  48.9 9.6 %scatter_fusion = f32[8,128,256]{2,1,0:T(8,128)} fusion(f32[8,128,256]{2,1,0:T(8,128)} %broadcast.803.clone, s32[32]{0:T(128)S(1)} %get-tuple-element.44, f32[32,128,256]{2,1,0:T(8,128)} %fusion.64), kind=kCustom, calls=%fused_computation.8 | custom fusion | flops 1048576 | bytes 12583040 | tf_op jit(solution)/shard_map/scatter-add | solution.py:45
  58.6 8.4 %collective-permute-start.6 = (f32[1024,256]{1,0:T(8,128)}, f32[1024,256]{1,0:T(8,128)}, u32[]{:S(2)}, u32[]{:S(2)}) collective-permute-start(f32[1024,256]{1,0:T(8,128)} %bitcast.36), channel_id=1, source_target_pairs={{8,0},{16,8},{24,16},{32,24},{40,32},{48,40},{56,48},{64,56},{72,6... | collective-permute-start | bytes 3145736 | tf_op jit(solution)/shard_map/ppermute | solution.py:16
  70.6 2.7 fusion.65
  73.4 6.5 scatter_fusion.1
  79.9 2.4 bitcast_add_fusion.2
  88.1 2.7 fusion.66
  90.9 6.5 scatter_fusion.2
  97.3 2.4 bitcast_add_fusion.1
  99.7 4.4 collective-permute-start.8
  107.3 2.3 broadcast_select_fusion.1
  109.8 2.7 fusion.67
  112.6 6.5 scatter_fusion.3
  120.4 2.8 collective-permute-start.9
  123.2 2.3 collective-permute-done.1
  126.6 4.1 collective-permute-start.2
  130.7 18.6 %collective-permute-done.2 = bf16[1024,256]{1,0:T(8,128)(2,1)} collective-permute-done((bf16[1024,256]{1,0:T(8,128)(2,1)S(1)}, bf16[1024,256]{1,0:T(8,128)(2,1)}, u32[]{:S(2)}, u32[]{:S(2)}) %collective-permute-start.2) | collective-permute-done | bytes 524320 | tf_op jit(solution)/shard_map/ppermute | solution.py:16
  149.4 13.5 %collective-permute-start.3 = (bf16[1024,256]{1,0:T(8,128)(2,1)S(1)}, bf16[1024,256]{1,0:T(8,128)(2,1)}, u32[]{:S(2)}, u32[]{:S(2)}) collective-permute-start(bf16[1024,256]{1,0:T(8,128)(2,1)S(1)} %broadcast_select_fusion.5), channel_id=1, source_target_pairs={{248,0},{0,8},{8,16},{16,24},{24,32},{32,40},{40,48},{48,56},{56,6... | collective-permute-start | bytes 1572872 | tf_op jit(solution)/shard_map/ppermute | solution.py:16
  164.1 4.9 collective-permute-done.3
  169.0 2.6 collective-permute-start.4
  173.6 3.3 bitcast_reduce_fusion.3
  178.7 9.5 %collective-permute-start.5 = (bf16[1024,256]{1,0:T(8,128)(2,1)}, bf16[1024,256]{1,0:T(8,128)(2,1)}, u32[]{:S(2)}, u32[]{:S(2)}) collective-permute-start(bf16[1024,256]{1,0:T(8,128)(2,1)} %collective-permute-done.4), channel_id=1, source_target_pairs={{248,0},{0,8},{8,16},{16,24},{24,32},{32,40},{40,48},{48,56},{56,6... | collective-permute-start | bytes 1572872 | tf_op jit(solution)/shard_map/ppermute | solution.py:16
  188.3 7.2 %collective-permute-done.10 = f32[1024,256]{1,0:T(8,128)} collective-permute-done((f32[1024,256]{1,0:T(8,128)}, f32[1024,256]{1,0:T(8,128)}, u32[]{:S(2)}, u32[]{:S(2)}) %collective-permute-start.10) | collective-permute-done | bytes 1048608 | tf_op jit(solution)/shard_map/ppermute | solution.py:16
  195.4 2.4 broadcast_select_fusion.2
  202.2 3.0 bitcast_reduce_fusion.1
  207.0 2.1 bitcast_reduce_fusion
  210.4 38.9 %collective-permute-done.11 = f32[1024,256]{1,0:T(8,128)} collective-permute-done((f32[1024,256]{1,0:T(8,128)}, f32[1024,256]{1,0:T(8,128)}, u32[]{:S(2)}, u32[]{:S(2)}) %collective-permute-start.11) | collective-permute-done | bytes 1048608 | tf_op jit(solution)/shard_map/ppermute | solution.py:16
  249.3 2.4 broadcast_select_fusion.4
  251.8 136.8 %all-reduce.6.cloned.1.call-done = (f32[1024,256]{1,0:T(8,128)}, f32[1024,256]{1,0:T(8,128)}) async-done(((f32[1024,256]{1,0:T(8,128)}, f32[1024,256]{1,0:T(8,128)}), (f32[1024,256]{1,0:T(8,128)}, f32[1024,256]{1,0:T(8,128)})) %all-reduce.6.cloned.1.call-update) | async-done | bytes 2097168 | tf_op jit(solution)/shard_map/psum | solution.py:50
  392.4 253.7 %all-reduce.4.cloned.1.call-done = f32[602,256]{1,0:T(8,128)} async-done(((f32[602,256]{1,0:T(8,128)}), f32[602,256]{1,0:T(8,128)}) %all-reduce.4.cloned.1.call-update) | async-done | bytes 616464 | tf_op jit(solution)/shard_map/psum | solution.py:98
  (90 shorter events, 40.7 us)
Async XLA Ops:
  7.2 75.1 %copy-start = (bf16[1024,602]{0,1:T(8,128)(2,1)S(1)}, bf16[1024,602]{0,1:T(8,128)(2,1)}, u32[]{:S(2)}) copy-start(bf16[1024,602]{0,1:T(8,128)(2,1)} %param.6) | copy-start | bytes 3698692
  7.2 381.5 %all-reduce.6.cloned.1.call-start = ((), (), s32[]{:S(2)}) async-start(), calls=%async_computation.1 | async-start | bytes 4194304 | tf_op jit(solution)/shard_map/psum | solution.py:50
  43.5 1.6 copy-start.3
  45.1 2.7 copy-start.5
  58.6 21.3 %collective-permute-start.6 = (f32[1024,256]{1,0:T(8,128)}, f32[1024,256]{1,0:T(8,128)}, u32[]{:S(2)}, u32[]{:S(2)}) collective-permute-start(f32[1024,256]{1,0:T(8,128)} %bitcast.36), channel_id=1, source_target_pairs={{8,0},{16,8},{24,16},{32,24},{40,32},{48,40},{56,48},{64,56},{72,6... | collective-permute-start | bytes 3145736 | tf_op jit(solution)/shard_map/ppermute | solution.py:16
  69.0 1.6 copy-start.4
  70.6 2.7 copy-start.6
  79.8 2.4 copy-start.14
  82.2 15.1 %collective-permute-start.7 = (f32[1024,256]{1,0:T(8,128)}, f32[1024,256]{1,0:T(8,128)}, u32[]{:S(2)}, u32[]{:S(2)}) collective-permute-start(f32[1024,256]{1,0:T(8,128)} %bitcast_add_fusion.2), channel_id=1, source_target_pairs={{8,0},{16,8},{24,16},{32,24},{40,32},{48,40},{56,48},{64,56},{72,6... | collective-permute-start | bytes 3145736 | tf_op jit(solution)/shard_map/ppermute | solution.py:16
  83.7 23.6 %collective-permute-start = (bf16[1024,256]{1,0:T(8,128)(2,1)}, bf16[1024,256]{1,0:T(8,128)(2,1)}, u32[]{:S(2)}, u32[]{:S(2)}) collective-permute-start(bf16[1024,256]{1,0:T(8,128)(2,1)} %fusion.24), channel_id=1, source_target_pairs={{224,0},{232,8},{240,16},{248,24},{0,32},{8,40},{16,48},{24,56},{3... | collective-permute-start | bytes 1572872 | tf_op jit(solution)/shard_map/ppermute | solution.py:16
  86.5 1.6 copy-start.2
  88.1 2.7 copy-start.7
  99.7 19.4 %collective-permute-start.8 = (f32[1024,256]{1,0:T(8,128)}, f32[1024,256]{1,0:T(8,128)}, u32[]{:S(2)}, u32[]{:S(2)}) collective-permute-start(f32[1024,256]{1,0:T(8,128)} %bitcast_add_fusion.1), channel_id=1, source_target_pairs={{8,0},{16,8},{24,16},{32,24},{40,32},{48,40},{56,48},{64,56},{72,6... | collective-permute-start | bytes 3145736 | tf_op jit(solution)/shard_map/ppermute | solution.py:16
  106.1 3.7 copy-start.1
  107.3 5.3 copy-start.9
  109.6 15.9 %collective-permute-start.1 = (bf16[1024,256]{1,0:T(8,128)(2,1)}, bf16[1024,256]{1,0:T(8,128)(2,1)}, u32[]{:S(2)}, u32[]{:S(2)}) collective-permute-start(bf16[1024,256]{1,0:T(8,128)(2,1)} %broadcast_select_fusion.1), channel_id=1, source_target_pairs={{192,0},{200,8},{208,16},{216,24},{224,32},{232,40},{240,48},{248,... | collective-permute-start | bytes 1572872 | tf_op jit(solution)/shard_map/ppermute | solution.py:16
  120.4 42.4 %collective-permute-start.9 = (f32[1024,256]{1,0:T(8,128)S(1)}, f32[1024,256]{1,0:T(8,128)}, u32[]{:S(2)}, u32[]{:S(2)}) collective-permute-start(f32[1024,256]{1,0:T(8,128)S(1)} %bitcast_add_fusion), channel_id=1, source_target_pairs={{32,0},{40,8},{48,16},{56,24},{64,32},{72,40},{80,48},{88,56},{96,... | collective-permute-start | bytes 3145736 | tf_op jit(solution)/shard_map/ppermute | solution.py:16
  126.6 22.7 %collective-permute-start.2 = (bf16[1024,256]{1,0:T(8,128)(2,1)S(1)}, bf16[1024,256]{1,0:T(8,128)(2,1)}, u32[]{:S(2)}, u32[]{:S(2)}) collective-permute-start(bf16[1024,256]{1,0:T(8,128)(2,1)S(1)} %broadcast_select_fusion.3), channel_id=1, source_target_pairs={{128,0},{136,8},{144,16},{152,24},{160,32},{168,40},{176,48},{184,... | collective-permute-start | bytes 1572872 | tf_op jit(solution)/shard_map/ppermute | solution.py:16
  149.4 19.6 %collective-permute-start.3 = (bf16[1024,256]{1,0:T(8,128)(2,1)S(1)}, bf16[1024,256]{1,0:T(8,128)(2,1)}, u32[]{:S(2)}, u32[]{:S(2)}) collective-permute-start(bf16[1024,256]{1,0:T(8,128)(2,1)S(1)} %broadcast_select_fusion.5), channel_id=1, source_target_pairs={{248,0},{0,8},{8,16},{16,24},{24,32},{32,40},{40,48},{48,56},{56,6... | collective-permute-start | bytes 1572872 | tf_op jit(solution)/shard_map/ppermute | solution.py:16
  164.1 31.3 %collective-permute-start.10 = (f32[1024,256]{1,0:T(8,128)}, f32[1024,256]{1,0:T(8,128)}, u32[]{:S(2)}, u32[]{:S(2)}) collective-permute-start(f32[1024,256]{1,0:T(8,128)} %broadcast_select_fusion), channel_id=1, source_target_pairs={{64,0},{72,8},{80,16},{88,24},{96,32},{104,40},{112,48},{120,56},{... | collective-permute-start | bytes 3145736 | tf_op jit(solution)/shard_map/ppermute | solution.py:16
  169.0 9.7 %collective-permute-start.4 = (bf16[1024,256]{1,0:T(8,128)(2,1)}, bf16[1024,256]{1,0:T(8,128)(2,1)}, u32[]{:S(2)}, u32[]{:S(2)}) collective-permute-start(bf16[1024,256]{1,0:T(8,128)(2,1)} %collective-permute-done.3), channel_id=1, source_target_pairs={{248,0},{0,8},{8,16},{16,24},{24,32},{32,40},{40,48},{48,56},{56,6... | collective-permute-start | bytes 1572872 | tf_op jit(solution)/shard_map/ppermute | solution.py:16
  171.6 2.0 copy-start.10
  178.7 20.1 %copy-start.8 = (bf16[32,128,128]{2,1,0:T(8,128)(2,1)S(1)}, bf16[32,128,128]{2,1,0:T(8,128)(2,1)}, u32[]{:S(2)}) copy-start(bf16[32,128,128]{2,1,0:T(8,128)(2,1)} %copy-done.7) | copy-start | bytes 3145732
  178.7 26.5 %collective-permute-start.5 = (bf16[1024,256]{1,0:T(8,128)(2,1)}, bf16[1024,256]{1,0:T(8,128)(2,1)}, u32[]{:S(2)}, u32[]{:S(2)}) collective-permute-start(bf16[1024,256]{1,0:T(8,128)(2,1)} %collective-permute-done.4), channel_id=1, source_target_pairs={{248,0},{0,8},{8,16},{16,24},{24,32},{32,40},{40,48},{48,56},{56,6... | collective-permute-start | bytes 1572872 | tf_op jit(solution)/shard_map/ppermute | solution.py:16
  197.8 51.5 %collective-permute-start.11 = (f32[1024,256]{1,0:T(8,128)}, f32[1024,256]{1,0:T(8,128)}, u32[]{:S(2)}, u32[]{:S(2)}) collective-permute-start(f32[1024,256]{1,0:T(8,128)} %broadcast_select_fusion.2), channel_id=1, source_target_pairs={{128,0},{136,8},{144,16},{152,24},{160,32},{168,40},{176,48},{184,... | collective-permute-start | bytes 3145736 | tf_op jit(solution)/shard_map/ppermute | solution.py:16
  206.9 2.2 copy-start.11
  207.0 2.2 copy-start.12
  207.0 2.2 copy-start.13
  210.4 178.2 %copy-start.16 = (bf16[128,256]{1,0:T(8,128)(2,1)S(1)}, bf16[128,256]{1,0:T(8,128)(2,1)}, u32[]{:S(2)}) copy-start(bf16[128,256]{1,0:T(8,128)(2,1)} %param.11) | copy-start | bytes 196612
  251.8 139.7 %copy-start.15 = (bf16[602,256]{1,0:T(8,128)(2,1)S(1)}, bf16[602,256]{1,0:T(8,128)(2,1)}, u32[]{:S(2)}) copy-start(bf16[602,256]{1,0:T(8,128)(2,1)} %param.7) | copy-start | bytes 924676
  251.8 394.3 %all-reduce.4.cloned.1.call-start = ((), (), s32[]{:S(2)}) async-start(), calls=%async_computation | async-start | bytes 1245184 | tf_op jit(solution)/shard_map/psum | solution.py:98
Sparse Core Ops, SparseCore 0:
  251.9 136.6 all-reduce.5
  394.7 251.3 all-reduce.3
where the time goes:
time: 657 us; the launch traced here: 655 us
  waiting for transfers between devices  462 us (70%)
  other arithmetic  53.7 us (8%)
  starting transfers between devices  47.3 us (7%)
  blocking collectives  30 us (5%)
  matrix products  29 us (4%)
  local copies, waits for them, and re-layouts  18 us (3%)
  between operations  14.4 us (2%)
    psum x1, waiting for transfers between devices, per_device(): grad_weight = lax.psum(partial_weight, ('loop', 'rep')) * total_scale  254 us
    psum x1, waiting for transfers between devices, reduce_rows(): summed = lax.psum(running, 'rep')  137 us
    ppermute x12, waiting for transfers between devices, shifted_2(): return lax.ppermute(block, axis, route)  71.9 us
    ppermute x12, starting transfers between devices, shifted_2(): return lax.ppermute(block, axis, route)  47.2 us
    all_gather x1, blocking collectives, per_device(): upstream = lax.all_gather(upstream_share, 'rep', axis=0, tiled=True)  30 us
    scatter-add x4, other arithmetic, backward_tiles(): jax.ops.segment_sum(products, index_row % ROW_TILES, num_segments=ROW_TILES)  29 us
  transfers between devices with their start and end apart: 14, of which 7 were waited for; matrix products, arithmetic and copies ran while one was open for 11% of the time, Pallas kernels for 0%

commit v1 on v0

v1 whole, which is shorter than its diff:
```python
import functools
import math

import jax
import jax.numpy as jnp
from jax import lax
from jax.experimental import pallas as pl
from jax.experimental.pallas import tpu as pltpu
from jax.sharding import PartitionSpec as P

MESH = pl.DeviceIdType.MESH
TILE = 128
HID = 256
OWN = 1024
F_IN = 602
F_PAD = 640
NZ = 8
F32 = jnp.float32
BF16 = jnp.bfloat16
VM = pl.BlockSpec(memory_space=pltpu.VMEM)
SM = pl.BlockSpec(memory_space=pltpu.SMEM)
VMEM_LIMIT = 56 * 1024 * 1024


def place():
    l = lax.axis_index("loop")
    r = lax.axis_index("rep")
    z, yl, k = l // 4, (l // 2) % 2, l % 2
    x, yh = r // 2, r % 2
    return z, yl, k, x, yh, r


def device(z, yl, k, r):
    return (z * 4 + yl * 2 + k, r)


def device_xy(z, k, x, y):
    return (z * 4 + (y % 2) * 2 + k, x * 2 + y // 2)


def remote(src, dst, send, recv, dev):
    return pltpu.make_async_remote_copy(
        src_ref=src, dst_ref=dst, send_sem=send, recv_sem=recv, device_id=dev, device_id_type=MESH
    )


def signal(sem, dev):
    pl.semaphore_signal(sem, inc=1, device_id=dev, device_id_type=MESH)


def gather_kernel(
    feat, weight, deg, cot, codes, tiles,
    xall, ut, got, ft, chunks, fpad,
    code_send, code_recv, u_send, u_recv, x_send, x_recv, f_send, f_recv,
):
    z, yl, k, x, yh, r = place()
    y = yh * 2 + yl
    q = yl * 2 + k
    mate = device(z, yl, 1 - k, r)
    y_up = device_xy(z, k, x, (y + 1) % 4)
    y_down = device_xy(z, k, x, (y + 3) % 4)

    barrier = pltpu.get_barrier_semaphore()
    signal(barrier, mate)
    signal(barrier, y_up)
    signal(barrier, y_down)

    def greet(i, carry):
        signal(barrier, device((z + i) % NZ, yl, k, r))
        return carry

    lax.fori_loop(1, NZ, greet, 0)

    def greet_sources(i, carry):
        zs, dz = i // 2, i % 2
        rs = (zs - z - dz + 2 * NZ) % NZ

        @pl.when(jnp.logical_not((zs == z) & (rs == r)))
        def _():
            signal(barrier, device(zs, yl, k, rs))

        return carry

    lax.fori_loop(0, 2 * NZ, greet_sources, 0)
    edge = jnp.where((r == 0) | (r == NZ - 1), 1, 0)

    for j in range(4):
        row = jnp.concatenate([tiles[j : j + 1, :], jnp.zeros((1, TILE - 32), jnp.int32)], axis=1)
        for t in range(8):
            chunks[t, j, 0:4, :] = codes[j, 4 * t : 4 * t + 4, :]
            chunks[t, j, 4:8, :] = jnp.broadcast_to(row, (4, TILE))

    root_rows = lax.rsqrt(deg[...].astype(F32))
    root_cols = root_rows.T
    own_root = lax.rsqrt(deg[pl.ds(r, 1), :].astype(F32))
    up = cot[...].astype(F32).T * own_root
    ut[z] = up.astype(BF16)

    pl.semaphore_wait(barrier, 26 - edge)

    def code_target(i):
        t, j = i // 4, i % 4
        zc = (z - r - jnp.where(j > q, 1, 0) + 2 * NZ) % NZ
        c4 = (q - j + 4) % 4
        return t, j, zc, c4

    def code_copy(i):
        t, j, zc, c4 = code_target(i)
        return remote(
            chunks.at[t, j], got.at[z, c4], code_send.at[i], code_recv.at[z * 4 + c4], device(zc, yl, k, t)
        )

    def send_codes(i, carry):
        t, j, zc, c4 = code_target(i)
        mine = (zc == z) & (t == r)

        @pl.when(mine)
        def _():
            got[z, c4] = chunks[t, j]

        @pl.when(jnp.logical_not(mine))
        def _():
            code_copy(i).start()

        return carry

    lax.fori_loop(0, 32, send_codes, 0)

    u_copies = []
    for d in (4, 3, 5, 2, 6, 1, 7):
        u_copies.append(
            remote(ut.at[z], ut.at[z], u_send.at[d], u_recv.at[d], device((z + d) % NZ, yl, k, r))
        )
        u_copies[-1].start()

    def project(first):
        for t in range(first, first + 4):
            rows = pl.ds(t * TILE, TILE)
            proj = jnp.dot(feat[rows, :], weight[...], preferred_element_type=F32)
            xall[q, rows, :] = (proj * root_cols[:, t : t + 1]).astype(BF16)

    low, high = pl.ds(0, 512), pl.ds(512, 512)
    project(0)
    x_up = remote(xall.at[q, low], xall.at[q, low], x_send.at[0], x_recv.at[0], y_up)
    x_up.start()
    project(4)
    x_down = remote(xall.at[q, high], xall.at[q, high], x_send.at[1], x_recv.at[1], y_down)
    x_down.start()
    x_mate = remote(xall.at[q], xall.at[q], x_send.at[2], x_recv.at[2], mate)
    x_mate.start()

    fpad[...] = jnp.zeros_like(fpad)
    fpad[:, 0:F_IN] = feat[pl.ds(pl.multiple_of(r * TILE, TILE), TILE), :]
    for b in range(F_PAD // TILE):
        block = fpad[:, b * TILE : (b + 1) * TILE].astype(F32)
        ft[k, b * TILE : (b + 1) * TILE, :] = block.T.astype(BF16)
    f_copy = remote(ft.at[k], ft.at[k], f_send, f_recv, mate)
    f_copy.start()

    other = (1 - yl) * 2 + k
    x_up.wait_recv()
    pass_low = remote(xall.at[other, low], xall.at[other, low], x_send.at[3], x_recv.at[3], mate)
    pass_low.start()
    x_down.wait_recv()
    pass_high = remote(xall.at[other, high], xall.at[other, high], x_send.at[4], x_recv.at[4], mate)
    pass_high.start()

    def wait_codes(i, carry):
        t, j, zc, c4 = code_target(i)

        @pl.when(jnp.logical_not((zc == z) & (t == r)))
        def _():
            code_copy(i).wait_send()

        zs, cs = i // 4, i % 4
        rs = ((4 * zs + q - 4 * z - cs + 64) % 32) // 4

        @pl.when(jnp.logical_not((zs == z) & (rs == r)))
        def _():
            remote(chunks.at[0, 0], got.at[zs, cs], code_send.at[i], code_recv.at[i], mate).wait_recv()

        return carry

    lax.fori_loop(0, 32, wait_codes, 0)
    for copy in u_copies:
        copy.wait()
    x_up.wait_send()
    x_down.wait_send()
    x_mate.wait()
    pass_low.wait()
    pass_high.wait()
    f_copy.wait()


def gather_call(feat, weight, deg, cot, codes, tiles):
    dma = pltpu.SemaphoreType.DMA
    return pl.pallas_call(
        gather_kernel,
        out_shape=(
            jax.ShapeDtypeStruct((4, OWN, HID), BF16),
            jax.ShapeDtypeStruct((NZ, HID, TILE), BF16),
            jax.ShapeDtypeStruct((NZ, 4, 8, TILE), jnp.int32),
            jax.ShapeDtypeStruct((2, F_PAD, TILE), BF16),
        ),
        in_specs=[VM] * 6,
        out_specs=(VM, VM, VM, VM),
        scratch_shapes=[
            pltpu.VMEM((8, 4, 8, TILE), jnp.int32),
            pltpu.VMEM((TILE, F_PAD), BF16),
            dma((32,)), dma((32,)), dma((8,)), dma((8,)), dma((5,)), dma((5,)), dma, dma,
        ],
        compiler_params=pltpu.CompilerParams(
            collective_id=0, has_side_effects=True, vmem_limit_bytes=VMEM_LIMIT
        ),
    )(feat, weight, deg, cot, codes, tiles)


def local_kernel(slots, got, xall, ut, bt, yout, tbuf, dense, utw):
    r = lax.axis_index("rep")
    lanes = lax.broadcasted_iota(jnp.int32, (TILE, TILE), 0)

    def build(i, carry):
        zs, c = i // 4, i % 4
        block = got[zs, c]
        for m in range(4):
            code = block[m : m + 1, :]
            rows = jnp.where(lanes == (code >> 7), 1.0, 0.0).astype(BF16)
            cols = jnp.where(lanes == (code & 127), 1.0, 0.0).astype(BF16)
            counts = lax.dot_general(rows, cols, (((1,), (1,)), ((), ())), preferred_element_type=F32)
            tbuf[i, m] = counts.astype(BF16)
        return carry

    lax.fori_loop(0, 32, build, 0, unroll=2)

    def fill(i, carry):
        zs, c = i // 4, i % 4
        spot = [slots[i, 4 * r + m] % 8 for m in range(4)]
        tbuf[i, 4] = jnp.zeros((TILE, TILE), BF16)
        for j in range(8):
            at = jnp.int32(4)
            for m in range(4):
                at = jnp.where(spot[m] == j, m, at)
            dense[c, pl.ds(pl.multiple_of(zs * TILE, TILE), TILE), j * TILE : (j + 1) * TILE] = tbuf[i, at]
        return carry

    lax.fori_loop(0, 32, fill, 0)
    for zs in range(NZ):
        utw[:, zs * TILE : (zs + 1) * TILE] = ut[zs]

    for c in range(4):
        ys, ks = c // 2, c % 2
        for xs in range(4):
            prod = jnp.dot(
                utw[...], dense[c, :, xs * 256 : (xs + 1) * 256], preferred_element_type=F32
            ).astype(BF16)
            for h in range(2):
                dest_y = 2 * h + ys
                piece = prod[:, h * TILE : (h + 1) * TILE]
                bt[ks, 0, xs, dest_y] = piece[0:TILE, :]
                bt[ks, 1, dest_y, xs] = piece[TILE:, :]

    def forward(i, carry):
        rows = pl.ds(pl.multiple_of(i * 256, 256), 256)
        total = jnp.dot(dense[0, rows, :], xall[0], preferred_element_type=F32)
        for c in range(1, 4):
            total = total + jnp.dot(dense[c, rows, :], xall[c], preferred_element_type=F32)
        yout[2 * i] = total[0:TILE].astype(BF16)
        yout[2 * i + 1] = total[TILE:].astype(BF16)
        return carry

    lax.fori_loop(0, 4, forward, 0)


def local_call(slots, got, xall, ut):
    return pl.pallas_call(
        local_kernel,
        out_shape=(
            jax.ShapeDtypeStruct((2, 2, 4, 4, TILE, TILE), BF16),
            jax.ShapeDtypeStruct((NZ, TILE, HID), BF16),
        ),
        in_specs=[SM, VM, VM, VM],
        out_specs=(VM, VM),
        scratch_shapes=[
            pltpu.VMEM((32, 5, TILE, TILE), BF16),
            pltpu.VMEM((4, OWN, OWN), BF16),
            pltpu.VMEM((HID, OWN), BF16),
        ],
        compiler_params=pltpu.CompilerParams(vmem_limit_bytes=VMEM_LIMIT),
    )(slots, got, xall, ut)


def reduce_kernel(
    scale, bt, ypart, xall, cot, deg, weight, ft,
    out, gin, gw,
    r_mate, s_part, r_one, p_part, r_two, r_fwd, ng, gpart, r_plane, r_z,
    m_send, m_recv, a_send, a_recv, b_send, b_recv, y_send, y_recv,
    n_send, n_recv, g_send, g_recv, z_send, z_recv, h_send, h_recv, e_send, e_recv,
):
    z, yl, k, x, yh, r = place()
    y = yh * 2 + yl
    q = yl * 2 + k
    mate = device(z, yl, 1 - k, r)
    spot = x * 4 + y

    barrier = pltpu.get_barrier_semaphore()
    signal(barrier, mate)

    def greet_z(i, carry):
        signal(barrier, device((z + i) % NZ, yl, k, r))
        return carry

    lax.fori_loop(1, NZ, greet_z, 0)

    def greet_plane(i, carry):
        signal(barrier, device_xy(z, k, (x + i // 4) % 4, (y + i) % 4))
        return carry

    lax.fori_loop(1, 16, greet_plane, 0)
    pl.semaphore_wait(barrier, 23)

    pending = []

    def send(src, dst, s, t, dev):
        copy = remote(src, dst, s, t, dev)
        copy.start()
        pending.append(copy)
        return copy

    order = (2, 1, 3, 0)
    here = (x, y)
    mates = {}
    for d in order:
        for h in range(2):
            at = (here[h] + d) % 4
            mates[h, d] = send(
                bt.at[1 - k, h, at], r_mate.at[h, at], m_send.at[h, d], m_recv.at[h, d], mate
            )
    fwd = [
        send(ypart.at[(z + d) % NZ], r_fwd.at[d], y_send.at[d], y_recv.at[d], device((z + d) % NZ, yl, k, r))
        for d in (4, 3, 5, 2, 6, 1, 7)
    ]

    ones = []
    for d in order:
        for h in range(2):
            at = (here[h] + d) % 4
            mates[h, d].wait_recv()
            s_part[h, at] = (bt[k, h, at].astype(F32) + r_mate[h, at].astype(F32)).astype(BF16)
            if d:
                dev = device_xy(z, k, (x + d) % 4, y) if h == 0 else device_xy(z, k, x, (y + d) % 4)
                ones.append(send(s_part.at[h, at], r_one.at[h, d], a_send.at[h, d], a_recv.at[h, d], dev))
    for copy in ones:
        copy.wait_recv()
    twos = []
    for d in order:
        for h in range(2):
            at = (here[1 - h] + d) % 4
            total = s_part[h, here[h], at].astype(F32)
            for e in range(1, 4):
                total = total + r_one[h, e, at].astype(F32)
            if d:
                p_part[h, d] = total.astype(BF16)
                dev = device_xy(z, k, x, (y + d) % 4) if h == 0 else device_xy(z, k, (x + d) % 4, y)
                twos.append(send(p_part.at[h, d], r_two.at[h, d], b_send.at[h, d], b_recv.at[h, d], dev))
            elif h == 0:
                top = total
            else:
                bottom = total

    for copy in twos:
        copy.wait_recv()
    for e in range(1, 4):
        top = top + r_two[0, e].astype(F32)
        bottom = bottom + r_two[1, e].astype(F32)
    own_root = lax.rsqrt(deg[pl.ds(r, 1), :].astype(F32))
    up = (cot[...].astype(F32).T * own_root).astype(BF16).astype(F32)
    back = jnp.concatenate([top, bottom], axis=0) + up
    node_grad = (back * own_root).astype(BF16).astype(F32)
    halves = (node_grad[0:TILE].T.astype(BF16), node_grad[TILE:].T.astype(BF16))

    @pl.when(k == 0)
    def _():
        ng[0, 0] = halves[0]
        ng[1, 0] = halves[1]

    @pl.when(k == 1)
    def _():
        ng[0, 1] = halves[0]
        ng[1, 1] = halves[1]

    swap = send(ng.at[1 - k, k], ng.at[1 - k, k], n_send, n_recv, mate)
    full = jnp.concatenate(halves, axis=1)
    gin[...] = lax.dot_general(
        full, weight[...], (((1,), (1,)), ((), ())), preferred_element_type=F32
    ).astype(BF16)
    swap.wait_recv()

    both_nodes = jnp.concatenate([ng[k, 0], ng[k, 1]], axis=0)
    both_feat = jnp.concatenate([ft[0], ft[1]], axis=1)
    gpart[...] = jnp.dot(both_feat, both_nodes, preferred_element_type=F32).reshape(16, F_PAD // 16, TILE)

    planes = []
    for i in (10, 9, 11, 6, 14, 2, 8, 5, 7, 13, 15, 1, 3, 4, 12):
        xs, ys = (x + i // 4) % 4, (y + i % 4) % 4
        planes.append(
            send(gpart.at[xs * 4 + ys], r_plane.at[i], g_send.at[i], g_recv.at[i], device_xy(z, k, xs, ys))
        )
    for copy in planes:
        copy.wait_recv()
    total = gpart[spot]
    for i in range(1, 16):
        total = total + r_plane[i]
    r_z[z] = total
    zs = []
    for d in (4, 3, 5, 2, 6, 1, 7):
        zs.append(send(r_z.at[z], r_z.at[z], z_send.at[d], z_recv.at[d], device((z + d) % NZ, yl, k, r)))
    for copy in zs:
        copy.wait_recv()
    total = r_z[0]
    for i in range(1, NZ):
        total = total + r_z[i]
    gw[k, spot] = total * scale
    spread = []
    for i in (10, 9, 11, 6, 14, 2, 8, 5, 7, 13, 15, 1, 3, 4, 12):
        xs, ys = (x + i // 4) % 4, (y + i % 4) % 4
        spread.append(
            send(gw.at[k, spot], gw.at[k, spot], h_send.at[i], h_recv.at[i], device_xy(z, k, xs, ys))
        )

    for copy in fwd:
        copy.wait_recv()
    rows = pl.ds(pl.multiple_of(r * TILE, TILE), TILE)
    total = ypart[z].astype(F32) + xall[q, rows, :].astype(F32)
    for d in range(1, NZ):
        total = total + r_fwd[d].astype(F32)
    root_col = jnp.broadcast_to(own_root, (8, TILE)).T
    out[...] = (total * root_col[:, 0:1]).astype(BF16)

    for copy in spread:
        copy.wait_recv()
    last = send(gw.at[k], gw.at[k], e_send, e_recv, mate)
    last.wait_recv()
    for copy in pending:
        copy.wait_send()


def reduce_call(scale, bt, ypart, xall, cot, deg, weight, ft):
    dma = pltpu.SemaphoreType.DMA
    chunk = F_PAD // 16
    return pl.pallas_call(
        functools.partial(reduce_kernel, scale),
        out_shape=(
            jax.ShapeDtypeStruct((TILE, HID), BF16),
            jax.ShapeDtypeStruct((TILE, F_IN), BF16),
            jax.ShapeDtypeStruct((2, 16, chunk, TILE), F32),
        ),
        in_specs=[VM] * 7,
        out_specs=(VM, VM, VM),
        scratch_shapes=[
            pltpu.VMEM((2, 4, 4, TILE, TILE), BF16),
            pltpu.VMEM((2, 4, 4, TILE, TILE), BF16),
            pltpu.VMEM((2, 4, 4, TILE, TILE), BF16),
            pltpu.VMEM((2, 4, TILE, TILE), BF16),
            pltpu.VMEM((2, 4, TILE, TILE), BF16),
            pltpu.VMEM((8, TILE, HID), BF16),
            pltpu.VMEM((2, 2, TILE, TILE), BF16),
            pltpu.VMEM((16, chunk, TILE), F32),
            pltpu.VMEM((16, chunk, TILE), F32),
            pltpu.VMEM((NZ, chunk, TILE), F32),
            dma((2, 4)), dma((2, 4)), dma((2, 4)), dma((2, 4)), dma((2, 4)), dma((2, 4)), dma((8,)), dma((8,)),
            dma, dma, dma((16,)), dma((16,)), dma((8,)), dma((8,)), dma((16,)), dma((16,)), dma, dma,
        ],
        compiler_params=pltpu.CompilerParams(
            collective_id=1, has_side_effects=True, vmem_limit_bytes=VMEM_LIMIT
        ),
    )(bt, ypart, xall, cot, deg, weight, ft)


def per_device(node_features, weight, degree, tile_index, edge_codes, cotangent):
    deg = degree.reshape(8, TILE)
    xall, ut, got, ft = gather_call(node_features, weight, deg, cotangent, edge_codes[0], tile_index[0])
    slots = got[:, :, 4, :].reshape(32, TILE)
    bt, ypart = local_call(slots, got, xall, ut)
    scale = 1.0 / math.sqrt(node_features.shape[0] * lax.axis_size("loop"))
    out, gin, gw = reduce_call(scale, bt, ypart, xall, cotangent, deg, weight, ft)
    gw = gw.reshape(2, F_PAD, TILE)
    grad_weight = jnp.concatenate([gw[0, :F_IN], gw[1, :F_IN]], axis=1)
    return (out, grad_weight, gin)


def solution(mesh):
    return jax.shard_map(
        per_device,
        mesh=mesh,
        in_specs=(
            P("loop", None),
            P(),
            P("loop"),
            P("loop", "rep", None),
            P("loop", "rep", None, None),
            P(("loop", "rep"), None),
        ),
        out_specs=(P(("loop", "rep"), None), P(), P(("loop", "rep"), None)),
        check_vma=False,
    )
```

time: 657 us -> 104 us (0.16)
  waiting for transfers between devices: 462 us -> 0 us
  Pallas kernels: 0 us -> 95.5 us
  other arithmetic: 53.7 us -> 0.87 us
  starting transfers between devices: 47.3 us -> 0 us
  blocking collectives: 30 us -> 0 us
  matrix products: 29 us -> 0 us
  between operations: 14.4 us -> 0.67 us
  local copies, waits for them, and re-layouts: 18 us -> 6.52 us
    psum x2 -> x0, waiting for transfers between devices: 391 us -> none  [the longest x1 254 us: per_device(): grad_weight = lax.psum(partial_weight, ('loop', 'rep')) * total_scale]
    pallas_call x0 -> x3, Pallas kernels: none -> 95.5 us  [the longest x1 51.1 us: reduce_call(): pl.pallas_call(functools.partial(reduce_kernel, scale), out_shape=(jax.Sh...]
    ppermute x12 -> x0, waiting for transfers between devices: 71.9 us -> none  [shifted_2(): return lax.ppermute(block, axis, route)]
    ppermute x12 -> x0, starting transfers between devices: 47.2 us -> none  [shifted_2(): return lax.ppermute(block, axis, route)]
    all_gather x1 -> x0, blocking collectives: 30 us -> none  [per_device(): upstream = lax.all_gather(upstream_share, 'rep', axis=0, tiled=True)]
    scatter-add x4 -> x0, other arithmetic: 29 us -> none  [backward_tiles(): jax.ops.segment_sum(products, index_row % ROW_TILES, num_segments=ROW_TILES)]
    dot_general x15 -> x0, matrix products: 29 us -> none  [the longest x4 10.9 us: backward_tiles(): jnp.einsum('sab,sah->sbh', tile_stack, pieces, preferred_element_type=jnp...]
    gather x8 -> x0, local copies, waits for them, and re-layouts: 15.2 us -> none  [the longest x4 8.05 us: backward_tiles(): pieces = source.reshape(ROW_TILES, TILE, width)[index_row // ROW_TILES]]
  transfers between devices with their start and end apart: 14 -> 0, of which waited for: 7 -> 0; matrix products, arithmetic and copies ran while one was open for 11% -> 0% of each run, Pallas kernels for 0% -> 0%
where the time goes in v1:
time: 104 us
  Pallas kernels  95.5 us (92%)
  local copies, waits for them, and re-layouts  6.52 us (6%)
    pallas_call x1, Pallas kernels, reduce_call(): pl.pallas_call(functools.partial(reduce_kernel, scale), out_shape=(jax.Sh...  51.1 us
    pallas_call x1, Pallas kernels, gather_call(): pl.pallas_call(gather_kernel, out_shape=(jax.ShapeDtypeStruct((4, OWN, HI...  28.8 us
    pallas_call x1, Pallas kernels, local_call(): pl.pallas_call(local_kernel, out_shape=(jax.ShapeDtypeStruct((2, 2, 4, 4,...  15.6 us
    unnamed x7, local copies, waits for them, and re-layouts  3.85 us

profile of v1, /device:TPU:1, one launch (start us, length us, event | category | flops | bytes accessed | tf_op | source)
XLA Modules:
  0.0 103.6 jit_solution(17311234312132640195)
XLA Ops:
  0.6 2.4 %copy.9.feat = bf16[1024,602]{1,0:T(8,128)(2,1)} copy(bf16[1024,602]{0,1:T(8,128)(2,1)} %param.6) | data formatting | bytes 2465792 | tf_op args[0]
  3.0 28.8 %shard_map.85 = (bf16[4,1024,256]{2,1,0:T(8,128)(2,1)}, bf16[8,256,128]{2,1,0:T(8,128)(2,1)}, s32[8,4,8,128]{3,2,1,0:T(8,128)}, bf16[2,640,128]{2,1,0:T(8,128)(2,1)}) custom-call(bf16[1024,602]{1,0:T(8,128)(2,1)} %copy.9.feat, bf16[602,256]{1,0:T(8,128)(2,1)} %weight.3, s32[8,128]{1,0:T(8,128)} %bitcast.12, bf16[128,256]{1,0:T(8,128)(2,1)} %cot.3, ...), custom_call_target="tpu_custom_call" | custom-call | tf_op jit(solution)/shard_map/pallas_call | solution.py:197
  31.9 1.5 %slice.9 = s32[8,4,1,128]{3,2,1,0:T(1,128)} slice(s32[8,4,8,128]{3,2,1,0:T(8,128)} %get-tuple-element.12.got), slice={[0:8], [0:4], [4:5], [0:128]} | slice | bytes 32768 | tf_op jit(solution)/shard_map/slice | solution.py:482
  33.4 15.6 %shard_map.86 = (bf16[2,2,4,4,128,128]{5,4,3,2,1,0:T(8,128)(2,1)}, bf16[8,128,256]{2,1,0:T(8,128)(2,1)}) custom-call(s32[32,128]{1,0:T(8,128)} %bitcast.10, s32[8,4,8,128]{3,2,1,0:T(8,128)} %get-tuple-element.12.got, bf16[4,1024,256]{2,1,0:T(8,128)(2,1)} %get-tuple-element.13.xall, bf16[8,256,128]{2,1,0:T(8,128)(2,1)} %get-tuple-element.14.ut), custom_call_target="tpu_custom_call" | custom-call | tf_op jit(solution)/shard_map/pallas_call | solution.py:275
  49.0 51.1 %shard_map.87 = (bf16[128,256]{1,0:T(8,128)(2,1)}, bf16[128,602]{1,0:T(8,128)(2,1)}, f32[2,16,40,128]{3,2,1,0:T(8,128)}) custom-call(bf16[2,2,4,4,128,128]{5,4,3,2,1,0:T(8,128)(2,1)} %get-tuple-element.15.bt, bf16[8,128,256]{2,1,0:T(8,128)(2,1)} %get-tuple-element.16.ypart, bf16[4,1024,256]{2,1,0:T(8,128)(2,1)} %get-tuple-element.13.xall, ...), custom_call_target="tpu_custom_call" | custom-call | tf_op jit(solution)/shard_map/pallas_call | solution.py:450
  100.1 0.0 copy-start
  100.1 0.0 copy-start.1
  100.1 1.1 %slice_bitcast_fusion.1 = (f32[602,128]{1,0:T(8,128)S(1)}, f32[602,128]{1,0:T(8,128)S(1)}) fusion(f32[2,640,128]{2,1,0:T(8,128)} %bitcast.9), kind=kLoop, calls=%fused_computation.2 | loop fusion | bytes 1232896 | tf_op jit(solution)/shard_map/squeeze | solution.py:487
  101.3 0.9 pad_maximum_fusion
  102.1 0.0 copy-done
  102.1 0.8 copy.10
  102.9 0.0 copy-done.1
  102.9 0.6 copy.12
Async XLA Ops:
  100.1 2.0 %copy-start = (bf16[128,602]{1,0:T(8,128)(2,1)S(1)}, bf16[128,602]{1,0:T(8,128)(2,1)}, u32[]{:S(2)}) copy-start(bf16[128,602]{1,0:T(8,128)(2,1)} %get-tuple-element.23) | copy-start | bytes 462340
  100.1 2.8 %copy-start.1 = (bf16[128,256]{1,0:T(8,128)(2,1)S(1)}, bf16[128,256]{1,0:T(8,128)(2,1)}, u32[]{:S(2)}) copy-start(bf16[128,256]{1,0:T(8,128)(2,1)} %get-tuple-element.29) | copy-start | bytes 196612

commit v2 on v0

v2 whole, which is shorter than its diff:
```python
import functools
import math

import jax
import jax.numpy as jnp
from jax import lax
from jax.experimental import pallas as pl
from jax.experimental.pallas import tpu as pltpu
from jax.sharding import PartitionSpec as P

MESH = pl.DeviceIdType.MESH
TILE = 128
HID = 256
OWN = 1024
F_IN = 602
F_PAD = 640
CHUNK = F_PAD // 16
NZ = 8
F32 = jnp.float32
BF16 = jnp.bfloat16
VM = pl.BlockSpec(memory_space=pltpu.VMEM)
VMEM_LIMIT = 56 * 1024 * 1024
Z_ORDER = (4, 3, 5, 2, 6, 1, 7)
PLANE_ORDER = (10, 9, 11, 6, 14, 2, 8, 5, 7, 13, 15, 1, 3, 4, 12)
RING_ORDER = (2, 1, 3)


def device(z, yl, k, r):
    return (z * 4 + yl * 2 + k, r)


def device_xy(z, k, x, y):
    return (z * 4 + (y % 2) * 2 + k, x * 2 + y // 2)


def remote(src, dst, send, recv, dev):
    return pltpu.make_async_remote_copy(
        src_ref=src, dst_ref=dst, send_sem=send, recv_sem=recv, device_id=dev, device_id_type=MESH
    )


def signal(sem, dev):
    pl.semaphore_signal(sem, inc=1, device_id=dev, device_id_type=MESH)


def layer_kernel(
    scale, feat, weight, deg, cot, codes, tiles,
    out, gin, gw,
    chunks, got, spots, slots, tbuf, dense, xall, fother, dother, ut, utw, db,
    ymate, r_y, ys, r_fwd, bt, r_one, p_part, r_two, gp, r_swap, gs, r_plane, r_z,
    slot_sem, code_send, code_recv, u_send, u_recv, v_send, v_recv, x_send, x_recv, f_send, f_recv,
    m_send, m_recv, y_send, y_recv, a_send, a_recv, b_send, b_recv,
    w_send, w_recv, g_send, g_recv, z_send, z_recv, h_send, h_recv, e_send, e_recv,
):
    l = lax.axis_index("loop")
    r = lax.axis_index("rep")
    z, yl, k = l // 4, (l // 2) % 2, l % 2
    x, yh = r // 2, r % 2
    y = yh * 2 + yl
    spot = x * 4 + y
    mate = device(z, yl, 1 - k, r)
    y_up = device_xy(z, k, x, (y + 1) % 4)
    y_down = device_xy(z, k, x, (y + 3) % 4)

    def code_source(i):
        kr, zs, cr = i // 16, (i // 2) % 8, i % 2
        ks = (k + kr) % 2
        owner = 4 * zs + 2 * yl + ks
        column = 4 * z + 2 * ((yl + cr) % 2) + k
        rs = ((owner - column + 32) % 32) // 4
        return zs, ks, rs, (zs == z) & (ks == k) & (rs == r)

    def code_target(i):
        t, j = i // 4, i % 4
        column = (l - 4 * r - j + 64) % 32
        zc, yc, kc = column // 4, (column // 2) % 2, column % 2
        slot = ((k - kc + 2) % 2) * 16 + z * 2 + (yc - yl + 2) % 2
        return t, j, zc, kc, slot, (zc == z) & (kc == k) & (t == r)

    barrier = pltpu.get_barrier_semaphore()
    signal(barrier, mate)

    def greet_z(i, carry):
        signal(barrier, device((z + i) % NZ, yl, k, r))
        return carry

    lax.fori_loop(1, NZ, greet_z, 0)

    def greet_plane(i, carry):
        signal(barrier, device_xy(z, k, (x + i // 4) % 4, (y + i) % 4))
        return carry

    lax.fori_loop(1, 16, greet_plane, 0)

    def greet_sources(i, carry):
        zs, ks, rs, mine = code_source(i)

        @pl.when(jnp.logical_not(mine))
        def _():
            signal(barrier, device(zs, yl, ks, rs))

        return carry

    lax.fori_loop(0, 32, greet_sources, 0)
    kept = jnp.where(r == 0, 1 + yl, jnp.where(r == NZ - 1, 1 - yl, 0))

    for j in range(4):
        row = jnp.concatenate([tiles[j : j + 1, :], jnp.zeros((1, TILE - 32), jnp.int32)], axis=1)
        for t in range(8):
            chunks[t, j, 0:4, :] = codes[j, 4 * t : 4 * t + 4, :]
            chunks[t, j, 4:8, :] = jnp.broadcast_to(row, (4, TILE))

    root_rows = lax.rsqrt(deg[...].astype(F32))
    root_cols = root_rows.T
    own_root = lax.rsqrt(deg[pl.ds(r, 1), :].astype(F32))
    ut[z] = (cot[...].astype(F32).T * own_root).astype(BF16)
    for t in range(8):
        rows = slice(t * TILE, (t + 1) * TILE)
        proj = lax.dot_general(
            feat[:, rows], weight[...], (((0,), (0,)), ((), ())), preferred_element_type=F32
        )
        xall[0, rows, :] = (proj * root_cols[:, t : t + 1]).astype(BF16)

    pl.semaphore_wait(barrier, 55 - kept)

    pending = []

    def send(src, dst, s, t, dev):
        copy = remote(src, dst, s, t, dev)
        copy.start()
        pending.append(copy)
        return copy

    def send_codes(i, carry):
        t, j, zc, kc, slot, mine = code_target(i)

        @pl.when(mine)
        def _():
            got[slot] = chunks[t, j]

        @pl.when(jnp.logical_not(mine))
        def _():
            remote(
                chunks.at[t, j], got.at[slot], code_send.at[i], code_recv.at[slot], device(zc, yl, kc, t)
            ).start()

        return carry

    lax.fori_loop(0, 32, send_codes, 0)
    us = {
        d: send(ut.at[z], ut.at[z], u_send.at[d], u_recv.at[d], device((z + d) % NZ, yl, k, r)) for d in Z_ORDER
    }
    vs = [send(ut.at[z], ut.at[NZ + z], v_send.at[0], v_recv.at[0], mate)]
    low, high = pl.ds(0, 512), pl.ds(512, 512)
    xs = [
        send(xall.at[0, low], xall.at[1, low], x_send.at[0], x_recv.at[0], y_up),
        send(xall.at[0, high], xall.at[1, high], x_send.at[1], x_recv.at[1], y_down),
    ]
    fs = [
        send(deg, dother, f_send.at[2], f_recv.at[2], y_up),
        send(feat.at[:, low], fother.at[:, low], f_send.at[0], f_recv.at[0], y_up),
        send(feat.at[:, high], fother.at[:, high], f_send.at[1], f_recv.at[1], y_down),
    ]

    def wait_codes(i, carry):
        zs, ks, rs, mine = code_source(i)

        @pl.when(jnp.logical_not(mine))
        def _():
            remote(chunks.at[0, 0], got.at[i], code_send.at[i], code_recv.at[i], mate).wait_recv()

        return carry

    lax.fori_loop(0, 32, wait_codes, 0)

    spots[...] = got[:, 4, :]
    slot_copy = pltpu.make_async_copy(spots, slots, slot_sem)
    slot_copy.start()

    lanes = lax.broadcasted_iota(jnp.int32, (TILE, TILE), 0)

    def build(i, carry):
        block = got[i]
        for m in range(4):
            code = block[m : m + 1, :]
            rows = jnp.where(lanes == (code >> 7), 1.0, 0.0).astype(BF16)
            cols = jnp.where(lanes == (code & 127), 1.0, 0.0).astype(BF16)
            counts = lax.dot_general(rows, cols, (((1,), (1,)), ((), ())), preferred_element_type=F32)
            tbuf[i, m] = counts.astype(BF16)
        tbuf[i, 4] = jnp.zeros((TILE, TILE), BF16)
        return carry

    lax.fori_loop(0, 32, build, 0, unroll=2)
    slot_copy.wait()

    def fill(i, carry):
        w, c = i // 2, i % 2
        at_m = [slots[i, 4 * r + m] % 8 for m in range(4)]
        for j in range(8):
            at = jnp.int32(4)
            for m in range(4):
                at = jnp.where(at_m[m] == j, m, at)
            dense[c, pl.ds(pl.multiple_of(w * TILE, TILE), TILE), j * TILE : (j + 1) * TILE] = tbuf[i, at]
        return carry

    lax.fori_loop(0, 32, fill, 0)

    for copy in xs:
        copy.wait_recv()

    def forward(i, carry):
        rows = pl.ds(pl.multiple_of(OWN + i * 512, 512), 512)
        total = jnp.dot(dense[0, rows, :], xall[0], preferred_element_type=F32)
        total = total + jnp.dot(dense[1, rows, :], xall[1], preferred_element_type=F32)
        ymate[pl.ds(4 * i, 4)] = total.astype(BF16).reshape(4, TILE, HID)
        return carry

    lax.fori_loop(0, 2, forward, 0)
    swap_y = send(ymate, r_y, m_send, m_recv, mate)

    def forward_own(i, carry):
        rows = pl.ds(pl.multiple_of(i * 512, 512), 512)
        total = jnp.dot(dense[0, rows, :], xall[0], preferred_element_type=F32)
        total = total + jnp.dot(dense[1, rows, :], xall[1], preferred_element_type=F32)
        ys[pl.ds(4 * i, 4)] = total.astype(BF16).reshape(4, TILE, HID)
        return carry

    lax.fori_loop(0, 2, forward_own, 0)

    for d in (1, 7, 2, 6, 3, 5, 4):
        us[d].wait_recv()
        at = (z - d + NZ) % NZ
        vs.append(send(ut.at[at], ut.at[NZ + at], v_send.at[d], v_recv.at[d], mate))

    swap_y.wait_recv()
    for i in range(NZ):
        ys[i] = (ys[i].astype(F32) + r_y[i].astype(F32)).astype(BF16)
    fwd = [
        send(ys.at[(z + d) % NZ], r_fwd.at[d], y_send.at[d], y_recv.at[d], device((z + d) % NZ, yl, k, r))
        for d in Z_ORDER
    ]

    for copy in vs:
        copy.wait_recv()
    for i in range(2 * NZ):
        utw[:, i * TILE : (i + 1) * TILE] = ut[i]
    fs[0].wait_recv()
    other_rows = lax.rsqrt(dother[...].astype(F32))
    for c in range(2):
        ysd = (yl + c) % 2
        roots = root_rows if c == 0 else other_rows
        for xd in range(4):
            columns = slice(xd * 256, (xd + 1) * 256)
            prod = jnp.dot(utw[...], dense[c, :, columns], preferred_element_type=F32)
            root = jnp.concatenate([roots[2 * xd : 2 * xd + 1], roots[2 * xd + 1 : 2 * xd + 2]], axis=1)
            db[c, :, columns] = (prod * root).astype(BF16)
            prod = prod.astype(BF16)
            for h in range(2):
                piece = prod[:, h * TILE : (h + 1) * TILE]
                bt[0, xd, 2 * h + ysd] = piece[0:TILE, :]
                bt[1, 2 * h + ysd, xd] = piece[TILE:, :]

    up = (cot[...].astype(F32).T * own_root).astype(BF16).astype(F32)
    mine = pl.ds(pl.multiple_of(r * TILE, TILE), TILE)
    db[0, :, mine] = (db[0, :, mine].astype(F32) + up * own_root).astype(BF16)

    for copy in fs[1:]:
        copy.wait_recv()
    nt = (((1,), (1,)), ((), ()))
    part = lax.dot_general(feat[...], db[0], nt, preferred_element_type=F32)
    part = part + lax.dot_general(fother[...], db[1], nt, preferred_element_type=F32)
    for h in range(2):
        gp[h, 0:F_IN, :] = part[:, h * TILE : (h + 1) * TILE]
        gp[h, F_IN:F_PAD, :] = jnp.zeros((F_PAD - F_IN, TILE), F32)
    swap = send(gp.at[1 - k], r_swap, w_send, w_recv, mate)
    swap.wait_recv()
    gs[...] = (gp[k] + r_swap[...]).reshape(16, CHUNK, TILE)

    planes = []
    for i in PLANE_ORDER:
        xd, yd = (x + i // 4) % 4, (y + i % 4) % 4
        planes.append(
            send(gs.at[xd * 4 + yd], r_plane.at[i], g_send.at[i], g_recv.at[i], device_xy(z, k, xd, yd))
        )

    here = (x, y)
    ones = []
    for d in RING_ORDER:
        for h in range(2):
            at = (here[h] + d) % 4
            dev = device_xy(z, k, (x + d) % 4, y) if h == 0 else device_xy(z, k, x, (y + d) % 4)
            ones.append(send(bt.at[h, at], r_one.at[h, d], a_send.at[h, d], a_recv.at[h, d], dev))

    for copy in planes:
        copy.wait_recv()
    total = gs[spot]
    for i in range(1, 16):
        total = total + r_plane[i]
    r_z[z] = total
    zs = [
        send(r_z.at[z], r_z.at[z], z_send.at[d], z_recv.at[d], device((z + d) % NZ, yl, k, r)) for d in Z_ORDER
    ]

    for copy in ones:
        copy.wait_recv()
    twos = []
    for d in RING_ORDER + (0,):
        for h in range(2):
            at = (here[1 - h] + d) % 4
            total = bt[h, here[h], at].astype(F32)
            for e in range(1, 4):
                total = total + r_one[h, e, at].astype(F32)
            if d:
                p_part[h, d] = total.astype(BF16)
                dev = device_xy(z, k, x, (y + d) % 4) if h == 0 else device_xy(z, k, (x + d) % 4, y)
                twos.append(send(p_part.at[h, d], r_two.at[h, d], b_send.at[h, d], b_recv.at[h, d], dev))
            elif h == 0:
                top = total
            else:
                bottom = total

    for copy in zs:
        copy.wait_recv()
    total = r_z[0]
    for i in range(1, NZ):
        total = total + r_z[i]
    gw[k, spot] = total * scale
    spread = []
    for i in PLANE_ORDER:
        xd, yd = (x + i // 4) % 4, (y + i % 4) % 4
        spread.append(
            send(gw.at[k, spot], gw.at[k, spot], h_send.at[i], h_recv.at[i], device_xy(z, k, xd, yd))
        )

    for copy in twos:
        copy.wait_recv()
    for e in range(1, 4):
        top = top + r_two[0, e].astype(F32)
        bottom = bottom + r_two[1, e].astype(F32)
    back = jnp.concatenate([top, bottom], axis=0) + up
    node_grad = (back * own_root).astype(BF16)
    gin[...] = jnp.dot(weight[...], node_grad, preferred_element_type=F32).astype(BF16)

    for copy in fwd:
        copy.wait_recv()
    total = ys[z].astype(F32) + xall[0, mine, :].astype(F32)
    for d in range(1, NZ):
        total = total + r_fwd[d].astype(F32)
    root_col = jnp.broadcast_to(own_root, (8, TILE)).T
    out[...] = (total * root_col[:, 0:1]).astype(BF16)

    for copy in spread:
        copy.wait_recv()
    last = send(gw.at[k], gw.at[k], e_send, e_recv, mate)

    def wait_code_sends(i, carry):
        t, j, zc, kc, slot, mine = code_target(i)

        @pl.when(jnp.logical_not(mine))
        def _():
            remote(chunks.at[t, j], got.at[slot], code_send.at[i], code_recv.at[slot], mate).wait_send()

        return carry

    lax.fori_loop(0, 32, wait_code_sends, 0)
    last.wait_recv()
    for copy in pending:
        copy.wait_send()


def layer_call(scale, feat, weight, deg, cot, codes, tiles):
    dma = pltpu.SemaphoreType.DMA
    vm = pltpu.VMEM
    i32 = jnp.int32
    scratch = [
        vm((8, 4, 8, TILE), i32), vm((32, 8, TILE), i32), vm((32, TILE), i32), pltpu.SMEM((32, TILE), i32),
        vm((32, 5, TILE, TILE), BF16), vm((2, 2 * OWN, OWN), BF16), vm((2, OWN, HID), BF16),
        vm((F_IN, OWN), BF16), vm((8, TILE), i32), vm((2 * NZ, HID, TILE), BF16),
        vm((HID, 2 * OWN), BF16), vm((2, HID, OWN), BF16),
        vm((NZ, TILE, HID), BF16), vm((NZ, TILE, HID), BF16), vm((NZ, TILE, HID), BF16), vm((NZ, TILE, HID), BF16),
        vm((2, 4, 4, TILE, TILE), BF16), vm((2, 4, 4, TILE, TILE), BF16),
        vm((2, 4, TILE, TILE), BF16), vm((2, 4, TILE, TILE), BF16),
        vm((2, F_PAD, TILE), F32), vm((F_PAD, TILE), F32), vm((16, CHUNK, TILE), F32), vm((16, CHUNK, TILE), F32),
        vm((NZ, CHUNK, TILE), F32),
        dma, dma((32,)), dma((32,)), dma((8,)), dma((8,)), dma((8,)), dma((8,)), dma((2,)), dma((2,)), dma((3,)), dma((3,)),
        dma, dma, dma((8,)), dma((8,)), dma((2, 4)), dma((2, 4)), dma((2, 4)), dma((2, 4)),
        dma, dma, dma((16,)), dma((16,)), dma((8,)), dma((8,)), dma((16,)), dma((16,)), dma, dma,
    ]
    return pl.pallas_call(
        functools.partial(layer_kernel, scale),
        out_shape=(
            jax.ShapeDtypeStruct((TILE, HID), BF16),
            jax.ShapeDtypeStruct((F_IN, TILE), BF16),
            jax.ShapeDtypeStruct((2, 16, CHUNK, TILE), F32),
        ),
        in_specs=[VM] * 6,
        out_specs=(VM, VM, VM),
        scratch_shapes=scratch,
        compiler_params=pltpu.CompilerParams(
            collective_id=0, has_side_effects=True, vmem_limit_bytes=VMEM_LIMIT
        ),
    )(feat, weight, deg, cot, codes, tiles)


def per_device(node_features, weight, degree, tile_index, edge_codes, cotangent):
    scale = 1.0 / math.sqrt(node_features.shape[0] * lax.axis_size("loop"))
    out, gin, gw = layer_call(
        scale, node_features.T, weight, degree.reshape(8, TILE), cotangent, edge_codes[0], tile_index[0]
    )
    gw = gw.reshape(2, F_PAD, TILE)
    grad_weight = jnp.concatenate([gw[0, :F_IN], gw[1, :F_IN]], axis=1)
    return (out, grad_weight, gin.T)


def solution(mesh):
    return jax.shard_map(
        per_device,
        mesh=mesh,
        in_specs=(
            P("loop", None),
            P(),
            P("loop"),
            P("loop", "rep", None),
            P("loop", "rep", None, None),
            P(("loop", "rep"), None),
        ),
        out_specs=(P(("loop", "rep"), None), P(), P(("loop", "rep"), None)),
        check_vma=False,
    )
```

time: 657 us -> 75.5 us (0.11)
  waiting for transfers between devices: 462 us -> 0 us
  Pallas kernels: 0 us -> 71.4 us
  other arithmetic: 53.7 us -> 0.87 us
  starting transfers between devices: 47.3 us -> 0 us
  blocking collectives: 30 us -> 0 us
  matrix products: 29 us -> 0 us
  local copies, waits for them, and re-layouts: 18 us -> 2.44 us
  between operations: 14.4 us -> 0.66 us
    psum x2 -> x0, waiting for transfers between devices: 391 us -> none  [the longest x1 254 us: per_device(): grad_weight = lax.psum(partial_weight, ('loop', 'rep')) * total_scale]
    ppermute x12 -> x0, waiting for transfers between devices: 71.9 us -> none  [shifted_2(): return lax.ppermute(block, axis, route)]
    pallas_call x0 -> x1, Pallas kernels: none -> 71.4 us  [layer_call(): pl.pallas_call(functools.partial(layer_kernel, scale), out_shape=(jax.Sha...]
    ppermute x12 -> x0, starting transfers between devices: 47.2 us -> none  [shifted_2(): return lax.ppermute(block, axis, route)]
    all_gather x1 -> x0, blocking collectives: 30 us -> none  [per_device(): upstream = lax.all_gather(upstream_share, 'rep', axis=0, tiled=True)]
    scatter-add x4 -> x0, other arithmetic: 29 us -> none  [backward_tiles(): jax.ops.segment_sum(products, index_row % ROW_TILES, num_segments=ROW_TILES)]
    dot_general x15 -> x0, matrix products: 29 us -> none  [the longest x4 10.9 us: backward_tiles(): jnp.einsum('sab,sah->sbh', tile_stack, pieces, preferred_element_type=jnp...]
    gather x8 -> x0, local copies, waits for them, and re-layouts: 15.2 us -> none  [the longest x4 8.05 us: backward_tiles(): pieces = source.reshape(ROW_TILES, TILE, width)[index_row // ROW_TILES]]
  transfers between devices with their start and end apart: 14 -> 0, of which waited for: 7 -> 0; matrix products, arithmetic and copies ran while one was open for 11% -> 0% of each run, Pallas kernels for 0% -> 0%
where the time goes in v2:
time: 75.5 us; the launch traced here: 75.4 us
  Pallas kernels  71.4 us (95%)
  local copies, waits for them, and re-layouts  2.44 us (3%)
  other arithmetic  0.87 us (1%)
    pallas_call x1, Pallas kernels, layer_call(): pl.pallas_call(functools.partial(layer_kernel, scale), out_shape=(jax.Sha...  71.4 us

profile of v2, /device:TPU:1, one launch (start us, length us, event | category | flops | bytes accessed | tf_op | source)
XLA Modules:
  0.0 75.4 jit_solution(109255555120711983)
XLA Ops:
  0.6 71.4 %shard_map.85 = (bf16[128,256]{1,0:T(8,128)(2,1)}, bf16[602,128]{1,0:T(8,128)(2,1)}, f32[2,16,40,128]{3,2,1,0:T(8,128)}) custom-call(bf16[602,1024]{1,0:T(8,128)(2,1)} %bitcast.10, bf16[602,256]{1,0:T(8,128)(2,1)} %weight.1, s32[8,128]{1,0:T(8,128)} %bitcast.14, bf16[128,256]{1,0:T(8,128)(2,1)} %cot.1, s32[4,32,128]{2,1,0:T(8,128)} %bitcast.13, s32[4,32]{1,0:T(4,128)} %bitcast.15), custom_call_target="tpu_custom_call" | custom-call | tf_op jit(solution)/shard_map/pallas_call | solution.py:389
  72.0 0.0 copy-start.1
  72.0 0.0 copy-start
  72.0 1.1 %slice_bitcast_fusion.1 = (f32[602,128]{1,0:T(8,128)S(1)}, f32[602,128]{1,0:T(8,128)S(1)}) fusion(f32[2,640,128]{2,1,0:T(8,128)} %bitcast.11), kind=kLoop, calls=%fused_computation.2 | loop fusion | bytes 1232896 | tf_op jit(solution)/shard_map/squeeze | solution.py:411
  73.2 0.9 %pad_maximum_fusion = f32[602,256]{1,0:T(8,128)} fusion(f32[602,128]{1,0:T(8,128)S(1)} %get-tuple-element.10, f32[602,128]{1,0:T(8,128)S(1)} %get-tuple-element.9), kind=kLoop, calls=%fused_computation | loop fusion | flops 154112 | bytes 1232896 | tf_op jit(solution)/shard_map/concatenate | solution.py:411
  74.1 0.0 copy-done.1
  74.1 0.6 copy.11
  74.7 0.0 copy-done
  74.7 0.7 copy.12
Async XLA Ops:
  72.0 2.0 %copy-start.1 = (bf16[128,256]{1,0:T(8,128)(2,1)S(1)}, bf16[128,256]{1,0:T(8,128)(2,1)}, u32[]{:S(2)}) copy-start(bf16[128,256]{1,0:T(8,128)(2,1)} %get-tuple-element.14) | copy-start | bytes 196612
  72.0 2.7 %copy-start = (bf16[602,128]{1,0:T(8,128)(2,1)S(1)}, bf16[602,128]{1,0:T(8,128)(2,1)}, u32[]{:S(2)}) copy-start(bf16[602,128]{1,0:T(8,128)(2,1)} %get-tuple-element.8) | copy-start | bytes 462340

commit v3 on v2

--- a/solution.py
+++ b/solution.py
@@ -46,9 +46,9 @@
 def layer_kernel(
     scale, feat, weight, deg, cot, codes, tiles,
     out, gin, gw,
-    chunks, got, spots, slots, tbuf, dense, xall, fother, dother, ut, utw, db,
+    pairs, relay, chunks, got, spots, slots, tbuf, dense, xall, fother, dother, ut, utw, db,
     ymate, r_y, ys, r_fwd, bt, r_one, p_part, r_two, gp, r_swap, gs, r_plane, r_z,
-    slot_sem, code_send, code_recv, u_send, u_recv, v_send, v_recv, x_send, x_recv, f_send, f_recv,
+    slot_sem, code_send, code_recv, c_send, c_recv, q_send, q_recv, u_send, u_recv, v_send, v_recv, x_send, x_recv, f_send, f_recv,
     m_send, m_recv, y_send, y_recv, a_send, a_recv, b_send, b_recv,
     w_send, w_recv, g_send, g_recv, z_send, z_recv, h_send, h_recv, e_send, e_recv,
 ):
@@ -62,20 +62,16 @@
     y_up = device_xy(z, k, x, (y + 1) % 4)
     y_down = device_xy(z, k, x, (y + 3) % 4)
 
-    def code_source(i):
-        kr, zs, cr = i // 16, (i // 2) % 8, i % 2
-        ks = (k + kr) % 2
-        owner = 4 * zs + 2 * yl + ks
-        column = 4 * z + 2 * ((yl + cr) % 2) + k
-        rs = ((owner - column + 32) % 32) // 4
-        return zs, ks, rs, (zs == z) & (ks == k) & (rs == r)
-
-    def code_target(i):
-        t, j = i // 4, i % 4
+    def code_source(i, rs):
+        ks, yc = (k + i // 2) % 2, (yl + i % 2) % 2
+        zs = (z + rs + jnp.where(2 * yl + ks - 2 * yc - k < 0, 1, 0)) % NZ
+        return zs, ks, (zs == z) & (ks == k)
+
+    def code_target(j):
         column = (l - 4 * r - j + 64) % 32
         zc, yc, kc = column // 4, (column // 2) % 2, column % 2
-        slot = ((k - kc + 2) % 2) * 16 + z * 2 + (yc - yl + 2) % 2
-        return t, j, zc, kc, slot, (zc == z) & (kc == k) & (t == r)
+        slot = ((k - kc + 2) % 2) * 2 + (yc - yl + 2) % 2
+        return zc, kc, slot, (zc == z) & (kc == k)
 
     barrier = pltpu.get_barrier_semaphore()
     signal(barrier, mate)
@@ -92,23 +88,19 @@
 
     lax.fori_loop(1, 16, greet_plane, 0)
 
-    def greet_sources(i, carry):
-        zs, ks, rs, mine = code_source(i)
+    for i in range(4):
+        zs, ks, mine = code_source(i, r)
 
         @pl.when(jnp.logical_not(mine))
         def _():
-            signal(barrier, device(zs, yl, ks, rs))
-
-        return carry
-
-    lax.fori_loop(0, 32, greet_sources, 0)
+            signal(barrier, device(zs, yl, ks, r))
+
     kept = jnp.where(r == 0, 1 + yl, jnp.where(r == NZ - 1, 1 - yl, 0))
 
     for j in range(4):
         row = jnp.concatenate([tiles[j : j + 1, :], jnp.zeros((1, TILE - 32), jnp.int32)], axis=1)
-        for t in range(8):
-            chunks[t, j, 0:4, :] = codes[j, 4 * t : 4 * t + 4, :]
-            chunks[t, j, 4:8, :] = jnp.broadcast_to(row, (4, TILE))
+        pairs[j, 0:32, :] = codes[j]
+        pairs[j, 32:40, :] = jnp.broadcast_to(row, (8, TILE))
 
     root_rows = lax.rsqrt(deg[...].astype(F32))
     root_cols = root_rows.T
@@ -121,7 +113,7 @@
         )
         xall[0, rows, :] = (proj * root_cols[:, t : t + 1]).astype(BF16)
 
-    pl.semaphore_wait(barrier, 55 - kept)
+    pl.semaphore_wait(barrier, 27 - kept)
 
     pending = []
 
@@ -131,22 +123,25 @@
         pending.append(copy)
         return copy
 
-    def send_codes(i, carry):
-        t, j, zc, kc, slot, mine = code_target(i)
+    def code_copy(j):
+        zc, kc, slot, mine = code_target(j)
+        copy = remote(pairs.at[j], relay.at[slot], code_send.at[j], code_recv.at[slot], device(zc, yl, kc, r))
+        return slot, mine, copy
+
+    for j in range(4):
+        slot, mine, copy = code_copy(j)
 
         @pl.when(mine)
         def _():
-            got[slot] = chunks[t, j]
+            relay[slot] = pairs[j]
 
         @pl.when(jnp.logical_not(mine))
         def _():
-            remote(
-                chunks.at[t, j], got.at[slot], code_send.at[i], code_recv.at[slot], device(zc, yl, kc, t)
-            ).start()
-
-        return carry
-
-    lax.fori_loop(0, 32, send_codes, 0)
+            copy.start()
+
+    quarter = pl.ds(pl.multiple_of(512 + x * TILE, TILE), TILE)
+    y_quarter = device_xy(z, k, x, (y + 1 + 2 * (x % 2)) % 4)
+    f_quarter = send(feat.at[:, quarter], fother.at[:, quarter], f_send.at[3], f_recv.at[3], y_quarter)
     us = {
         d: send(ut.at[z], ut.at[z], u_send.at[d], u_recv.at[d], device((z + d) % NZ, yl, k, r)) for d in Z_ORDER
     }
@@ -156,22 +151,39 @@
         send(xall.at[0, low], xall.at[1, low], x_send.at[0], x_recv.at[0], y_up),
         send(xall.at[0, high], xall.at[1, high], x_send.at[1], x_recv.at[1], y_down),
     ]
+    f_low, f_high = pl.ds(0, 256), pl.ds(256, 256)
     fs = [
         send(deg, dother, f_send.at[2], f_recv.at[2], y_up),
-        send(feat.at[:, low], fother.at[:, low], f_send.at[0], f_recv.at[0], y_up),
-        send(feat.at[:, high], fother.at[:, high], f_send.at[1], f_recv.at[1], y_down),
+        send(feat.at[:, f_low], fother.at[:, f_low], f_send.at[0], f_recv.at[0], y_up),
+        send(feat.at[:, f_high], fother.at[:, f_high], f_send.at[1], f_recv.at[1], y_down),
     ]
 
-    def wait_codes(i, carry):
-        zs, ks, rs, mine = code_source(i)
+    for i in range(4):
+        zs, ks, mine = code_source(i, r)
 
         @pl.when(jnp.logical_not(mine))
         def _():
-            remote(chunks.at[0, 0], got.at[i], code_send.at[i], code_recv.at[i], mate).wait_recv()
-
-        return carry
-
-    lax.fori_loop(0, 32, wait_codes, 0)
+            remote(pairs.at[0], relay.at[i], code_send.at[i], code_recv.at[i], mate).wait_recv()
+
+    for i in range(4):
+        for t in range(8):
+            chunks[t, i, 0:4, :] = relay[i, 4 * t : 4 * t + 4, :]
+            chunks[t, i, 4:8, :] = relay[i, 32:36, :]
+    cs = []
+    for d in (3, 5, 1, 7, 2, 6, 4):
+        t = (r + d) % 8
+        cs.append(send(chunks.at[t], got.at[pl.ds(4 * r, 4)], c_send.at[d], c_recv.at[d], (l, t)))
+    got[pl.ds(4 * r, 4)] = chunks[r]
+    f_quarter.wait_recv()
+    for d in RING_ORDER:
+        fs.append(
+            send(
+                fother.at[:, quarter], fother.at[:, quarter], q_send.at[d], q_recv.at[d],
+                device_xy(z, k, (x + d) % 4, y),
+            )
+        )
+    for copy in cs:
+        copy.wait_recv()
 
     spots[...] = got[:, 4, :]
     slot_copy = pltpu.make_async_copy(spots, slots, slot_sem)
@@ -190,11 +202,12 @@
         tbuf[i, 4] = jnp.zeros((TILE, TILE), BF16)
         return carry
 
-    lax.fori_loop(0, 32, build, 0, unroll=2)
+    lax.fori_loop(0, 32, build, 0, unroll=4)
     slot_copy.wait()
 
     def fill(i, carry):
-        w, c = i // 2, i % 2
+        zs, _, _ = code_source(i % 4, i // 4)
+        w, c = ((i // 2) % 2) * NZ + zs, i % 2
         at_m = [slots[i, 4 * r + m] % 8 for m in range(4)]
         for j in range(8):
             at = jnp.int32(4)
@@ -205,40 +218,10 @@
 
     lax.fori_loop(0, 32, fill, 0)
 
-    for copy in xs:
-        copy.wait_recv()
-
-    def forward(i, carry):
-        rows = pl.ds(pl.multiple_of(OWN + i * 512, 512), 512)
-        total = jnp.dot(dense[0, rows, :], xall[0], preferred_element_type=F32)
-        total = total + jnp.dot(dense[1, rows, :], xall[1], preferred_element_type=F32)
-        ymate[pl.ds(4 * i, 4)] = total.astype(BF16).reshape(4, TILE, HID)
-        return carry
-
-    lax.fori_loop(0, 2, forward, 0)
-    swap_y = send(ymate, r_y, m_send, m_recv, mate)
-
-    def forward_own(i, carry):
-        rows = pl.ds(pl.multiple_of(i * 512, 512), 512)
-        total = jnp.dot(dense[0, rows, :], xall[0], preferred_element_type=F32)
-        total = total + jnp.dot(dense[1, rows, :], xall[1], preferred_element_type=F32)
-        ys[pl.ds(4 * i, 4)] = total.astype(BF16).reshape(4, TILE, HID)
-        return carry
-
-    lax.fori_loop(0, 2, forward_own, 0)
-
     for d in (1, 7, 2, 6, 3, 5, 4):
         us[d].wait_recv()
         at = (z - d + NZ) % NZ
         vs.append(send(ut.at[at], ut.at[NZ + at], v_send.at[d], v_recv.at[d], mate))
-
-    swap_y.wait_recv()
-    for i in range(NZ):
-        ys[i] = (ys[i].astype(F32) + r_y[i].astype(F32)).astype(BF16)
-    fwd = [
-        send(ys.at[(z + d) % NZ], r_fwd.at[d], y_send.at[d], y_recv.at[d], device((z + d) % NZ, yl, k, r))
-        for d in Z_ORDER
-    ]
 
     for copy in vs:
         copy.wait_recv()
@@ -291,6 +274,36 @@
             dev = device_xy(z, k, (x + d) % 4, y) if h == 0 else device_xy(z, k, x, (y + d) % 4)
             ones.append(send(bt.at[h, at], r_one.at[h, d], a_send.at[h, d], a_recv.at[h, d], dev))
 
+    for copy in xs:
+        copy.wait_recv()
+
+    def forward(i, carry):
+        rows = pl.ds(pl.multiple_of(OWN + i * 512, 512), 512)
+        total = jnp.dot(dense[0, rows, :], xall[0], preferred_element_type=F32)
+        total = total + jnp.dot(dense[1, rows, :], xall[1], preferred_element_type=F32)
+        ymate[pl.ds(4 * i, 4)] = total.astype(BF16).reshape(4, TILE, HID)
+        return carry
+
+    lax.fori_loop(0, 2, forward, 0)
+    swap_y = send(ymate, r_y, m_send, m_recv, mate)
+
+    def forward_own(i, carry):
+        rows = pl.ds(pl.multiple_of(i * 512, 512), 512)
+        total = jnp.dot(dense[0, rows, :], xall[0], preferred_element_type=F32)
+        total = total + jnp.dot(dense[1, rows, :], xall[1], preferred_element_type=F32)
+        ys[pl.ds(4 * i, 4)] = total.astype(BF16).reshape(4, TILE, HID)
+        return carry
+
+    lax.fori_loop(0, 2, forward_own, 0)
+
+    swap_y.wait_recv()
+    for i in range(NZ):
+        ys[i] = (ys[i].astype(F32) + r_y[i].astype(F32)).astype(BF16)
+    fwd = [
+        send(ys.at[(z + d) % NZ], r_fwd.at[d], y_send.at[d], y_recv.at[d], device((z + d) % NZ, yl, k, r))
+        for d in Z_ORDER
+    ]
+
     for copy in planes:
         copy.wait_recv()
     total = gs[spot]
@@ -324,12 +337,13 @@
     total = r_z[0]
     for i in range(1, NZ):
         total = total + r_z[i]
-    gw[k, spot] = total * scale
+    half = pl.ds(pl.multiple_of(k * TILE, TILE), TILE)
+    gw[spot, :, half] = total * scale
     spread = []
     for i in PLANE_ORDER:
         xd, yd = (x + i // 4) % 4, (y + i % 4) % 4
         spread.append(
-            send(gw.at[k, spot], gw.at[k, spot], h_send.at[i], h_recv.at[i], device_xy(z, k, xd, yd))
+            send(gw.at[spot, :, half], gw.at[spot, :, half], h_send.at[i], h_recv.at[i], device_xy(z, k, xd, yd))
         )
 
     for copy in twos:
@@ -351,18 +365,15 @@
 
     for copy in spread:
         copy.wait_recv()
-    last = send(gw.at[k], gw.at[k], e_send, e_recv, mate)
-
-    def wait_code_sends(i, carry):
-        t, j, zc, kc, slot, mine = code_target(i)
+    last = send(gw.at[:, :, half], gw.at[:, :, half], e_send, e_recv, mate)
+
+    for j in range(4):
+        _, mine, copy = code_copy(j)
 
         @pl.when(jnp.logical_not(mine))
         def _():
-            remote(chunks.at[t, j], got.at[slot], code_send.at[i], code_recv.at[slot], mate).wait_send()
-
-        return carry
-
-    lax.fori_loop(0, 32, wait_code_sends, 0)
+            copy.wait_send()
+
     last.wait_recv()
     for copy in pending:
         copy.wait_send()
@@ -373,7 +384,7 @@
     vm = pltpu.VMEM
     i32 = jnp.int32
     scratch = [
-        vm((8, 4, 8, TILE), i32), vm((32, 8, TILE), i32), vm((32, TILE), i32), pltpu.SMEM((32, TILE), i32),
+        vm((4, 40, TILE), i32), vm((4, 40, TILE), i32), vm((8, 4, 8, TILE), i32), vm((32, 8, TILE), i32), vm((32, TILE), i32), pltpu.SMEM((32, TILE), i32),
         vm((32, 5, TILE, TILE), BF16), vm((2, 2 * OWN, OWN), BF16), vm((2, OWN, HID), BF16),
         vm((F_IN, OWN), BF16), vm((8, TILE), i32), vm((2 * NZ, HID, TILE), BF16),
         vm((HID, 2 * OWN), BF16), vm((2, HID, OWN), BF16),
@@ -382,7 +393,8 @@
         vm((2, 4, TILE, TILE), BF16), vm((2, 4, TILE, TILE), BF16),
         vm((2, F_PAD, TILE), F32), vm((F_PAD, TILE), F32), vm((16, CHUNK, TILE), F32), vm((16, CHUNK, TILE), F32),
         vm((NZ, CHUNK, TILE), F32),
-        dma, dma((32,)), dma((32,)), dma((8,)), dma((8,)), dma((8,)), dma((8,)), dma((2,)), dma((2,)), dma((3,)), dma((3,)),
+        dma, dma((4,)), dma((4,)), dma((8,)), dma((8,)), dma((4,)), dma((4,)),
+        dma((8,)), dma((8,)), dma((8,)), dma((8,)), dma((2,)), dma((2,)), dma((4,)), dma((4,)),
         dma, dma, dma((8,)), dma((8,)), dma((2, 4)), dma((2, 4)), dma((2, 4)), dma((2, 4)),
         dma, dma, dma((16,)), dma((16,)), dma((8,)), dma((8,)), dma((16,)), dma((16,)), dma, dma,
     ]
@@ -391,7 +403,7 @@
         out_shape=(
             jax.ShapeDtypeStruct((TILE, HID), BF16),
             jax.ShapeDtypeStruct((F_IN, TILE), BF16),
-            jax.ShapeDtypeStruct((2, 16, CHUNK, TILE), F32),
+            jax.ShapeDtypeStruct((16, CHUNK, HID), F32),
         ),
         in_specs=[VM] * 6,
         out_specs=(VM, VM, VM),
@@ -407,9 +419,7 @@
     out, gin, gw = layer_call(
         scale, node_features.T, weight, degree.reshape(8, TILE), cotangent, edge_codes[0], tile_index[0]
     )
-    gw = gw.reshape(2, F_PAD, TILE)
-    grad_weight = jnp.concatenate([gw[0, :F_IN], gw[1, :F_IN]], axis=1)
-    return (out, grad_weight, gin.T)
+    return (out, gw.reshape(F_PAD, HID)[:F_IN], gin.T)
 
 
 def solution(mesh):

time: 75.5 us -> 81.1 us (1.074)
  Pallas kernels: 71.4 us -> 77 us
  other arithmetic: 0.87 us -> 0 us
  local copies, waits for them, and re-layouts: 2.44 us -> 3.28 us
    pallas_call x1, Pallas kernels: 71.4 us -> 77 us  [layer_call(): pl.pallas_call(functools.partial(layer_kernel, scale), out_shape=(jax.Sha...]
    slice x0 -> x1, local copies, waits for them, and re-layouts: none -> 1.98 us  [per_device(): return (out, gw.reshape(F_PAD, HID)[:F_IN], gin.T)]
    squeeze x1 -> x0, local copies, waits for them, and re-layouts: 1.14 us -> none  [per_device(): grad_weight = jnp.concatenate([gw[0, :F_IN], gw[1, :F_IN]], axis=1)]
    concatenate x1 -> x0, other arithmetic: 0.87 us -> none  [per_device(): grad_weight = jnp.concatenate([gw[0, :F_IN], gw[1, :F_IN]], axis=1)]
where the time goes in v3:
time: 81.1 us; the launch traced here: 80.9 us
  Pallas kernels  77 us (95%)
  local copies, waits for them, and re-layouts  3.28 us (4%)
    pallas_call x1, Pallas kernels, layer_call(): pl.pallas_call(functools.partial(layer_kernel, scale), out_shape=(jax.Sha...  77 us
    slice x1, local copies, waits for them, and re-layouts, per_device(): return (out, gw.reshape(F_PAD, HID)[:F_IN], gin.T)  1.98 us

profile of v3, /device:TPU:1, one launch (start us, length us, event | category | flops | bytes accessed | tf_op | source)
XLA Modules:
  0.0 80.9 jit_solution(17783693296624202714)
XLA Ops:
  0.6 77.0 %shard_map.85 = (bf16[128,256]{1,0:T(8,128)(2,1)}, bf16[602,128]{1,0:T(8,128)(2,1)}, f32[16,40,256]{2,1,0:T(8,128)}) custom-call(bf16[602,1024]{1,0:T(8,128)(2,1)} %bitcast.6, bf16[602,256]{1,0:T(8,128)(2,1)} %weight.1, s32[8,128]{1,0:T(8,128)} %bitcast.10, bf16[128,256]{1,0:T(8,128)(2,1)} %cot.1, s32[4,32,128]{2,1,0:T(8,128)} %bitcast.9, s32[4,32]{1,0:T(4,128)} %bitcast.11), custom_call_target="tpu_custom_call" | custom-call | tf_op jit(solution)/shard_map/pallas_call | solution.py:401
  77.6 0.0 copy-start.1
  77.6 0.0 copy-start
  77.6 2.0 %slice.4 = f32[602,256]{1,0:T(8,128)} slice(f32[640,256]{1,0:T(8,128)} %bitcast.7), slice={[0:602], [0:256]} | slice | bytes 1232896 | tf_op jit(solution)/shard_map/slice | solution.py:422
  79.6 0.0 copy-done.1
  79.6 0.6 copy.11
  80.3 0.0 copy-done
  80.3 0.7 copy.12
Async XLA Ops:
  77.6 2.0 %copy-start.1 = (bf16[128,256]{1,0:T(8,128)(2,1)S(1)}, bf16[128,256]{1,0:T(8,128)(2,1)}, u32[]{:S(2)}) copy-start(bf16[128,256]{1,0:T(8,128)(2,1)} %get-tuple-element.12) | copy-start | bytes 196612
  77.6 2.6 %copy-start = (bf16[602,128]{1,0:T(8,128)(2,1)S(1)}, bf16[602,128]{1,0:T(8,128)(2,1)}, u32[]{:S(2)}) copy-start(bf16[602,128]{1,0:T(8,128)(2,1)} %get-tuple-element.8) | copy-start | bytes 462340

commit v4 on v3

--- a/solution.py
+++ b/solution.py
@@ -44,11 +44,11 @@
 
 
 def layer_kernel(
-    scale, feat, weight, deg, cot, codes, tiles,
+    scale, feat_hbm, weight, deg, cot, codes, tiles,
     out, gin, gw,
-    pairs, relay, chunks, got, spots, slots, tbuf, dense, xall, fother, dother, ut, utw, db,
+    feat, pairs, relay, chunks, got, spots, slots, tbuf, dense, xall, fother, dother, ut, utw, db,
     ymate, r_y, ys, r_fwd, bt, r_one, p_part, r_two, gp, r_swap, gs, r_plane, r_z,
-    slot_sem, code_send, code_recv, c_send, c_recv, q_send, q_recv, u_send, u_recv, v_send, v_recv, x_send, x_recv, f_send, f_recv,
+    feat_sem, slot_sem, code_send, code_recv, c_send, c_recv, q_send, q_recv, u_send, u_recv, v_send, v_recv, x_send, x_recv, f_send, f_recv,
     m_send, m_recv, y_send, y_recv, a_send, a_recv, b_send, b_recv,
     w_send, w_recv, g_send, g_recv, z_send, z_recv, h_send, h_recv, e_send, e_recv,
 ):
@@ -73,6 +73,8 @@
         slot = ((k - kc + 2) % 2) * 2 + (yc - yl + 2) % 2
         return zc, kc, slot, (zc == z) & (kc == k)
 
+    stage = pltpu.make_async_copy(feat_hbm, feat, feat_sem)
+    stage.start()
     barrier = pltpu.get_barrier_semaphore()
     signal(barrier, mate)
 
@@ -106,6 +108,7 @@
     root_cols = root_rows.T
     own_root = lax.rsqrt(deg[pl.ds(r, 1), :].astype(F32))
     ut[z] = (cot[...].astype(F32).T * own_root).astype(BF16)
+    stage.wait()
     for t in range(8):
         rows = slice(t * TILE, (t + 1) * TILE)
         proj = lax.dot_general(
@@ -142,6 +145,21 @@
     quarter = pl.ds(pl.multiple_of(512 + x * TILE, TILE), TILE)
     y_quarter = device_xy(z, k, x, (y + 1 + 2 * (x % 2)) % 4)
     f_quarter = send(feat.at[:, quarter], fother.at[:, quarter], f_send.at[3], f_recv.at[3], y_quarter)
+    for i in range(4):
+        zs, ks, mine = code_source(i, r)
+
+        @pl.when(jnp.logical_not(mine))
+        def _():
+            remote(pairs.at[0], relay.at[i], code_send.at[i], code_recv.at[i], mate).wait_recv()
+
+    for i in range(4):
+        for t in range(8):
+            chunks[t, i, 0:4, :] = relay[i, 4 * t : 4 * t + 4, :]
+            chunks[t, i, 4:8, :] = relay[i, 32:36, :]
+    cs = []
+    for d in (3, 5, 1, 7, 2, 6, 4):
+        t = (r + d) % 8
+        cs.append(send(chunks.at[t], got.at[pl.ds(4 * r, 4)], c_send.at[d], c_recv.at[d], (l, t)))
     us = {
         d: send(ut.at[z], ut.at[z], u_send.at[d], u_recv.at[d], device((z + d) % NZ, yl, k, r)) for d in Z_ORDER
     }
@@ -158,21 +176,6 @@
         send(feat.at[:, f_high], fother.at[:, f_high], f_send.at[1], f_recv.at[1], y_down),
     ]
 
-    for i in range(4):
-        zs, ks, mine = code_source(i, r)
-
-        @pl.when(jnp.logical_not(mine))
-        def _():
-            remote(pairs.at[0], relay.at[i], code_send.at[i], code_recv.at[i], mate).wait_recv()
-
-    for i in range(4):
-        for t in range(8):
-            chunks[t, i, 0:4, :] = relay[i, 4 * t : 4 * t + 4, :]
-            chunks[t, i, 4:8, :] = relay[i, 32:36, :]
-    cs = []
-    for d in (3, 5, 1, 7, 2, 6, 4):
-        t = (r + d) % 8
-        cs.append(send(chunks.at[t], got.at[pl.ds(4 * r, 4)], c_send.at[d], c_recv.at[d], (l, t)))
     got[pl.ds(4 * r, 4)] = chunks[r]
     f_quarter.wait_recv()
     for d in RING_ORDER:
@@ -202,7 +205,7 @@
         tbuf[i, 4] = jnp.zeros((TILE, TILE), BF16)
         return carry
 
-    lax.fori_loop(0, 32, build, 0, unroll=4)
+    lax.fori_loop(0, 32, build, 0, unroll=8)
     slot_copy.wait()
 
     def fill(i, carry):
@@ -218,10 +221,40 @@
 
     lax.fori_loop(0, 32, fill, 0)
 
+    for copy in xs:
+        copy.wait_recv()
+
+    def forward(i, carry):
+        rows = pl.ds(pl.multiple_of(OWN + i * 512, 512), 512)
+        total = jnp.dot(dense[0, rows, :], xall[0], preferred_element_type=F32)
+        total = total + jnp.dot(dense[1, rows, :], xall[1], preferred_element_type=F32)
+        ymate[pl.ds(4 * i, 4)] = total.astype(BF16).reshape(4, TILE, HID)
+        return carry
+
+    lax.fori_loop(0, 2, forward, 0)
+    swap_y = send(ymate, r_y, m_send, m_recv, mate)
+
+    def forward_own(i, carry):
+        rows = pl.ds(pl.multiple_of(i * 512, 512), 512)
+        total = jnp.dot(dense[0, rows, :], xall[0], preferred_element_type=F32)
+        total = total + jnp.dot(dense[1, rows, :], xall[1], preferred_element_type=F32)
+        ys[pl.ds(4 * i, 4)] = total.astype(BF16).reshape(4, TILE, HID)
+        return carry
+
+    lax.fori_loop(0, 2, forward_own, 0)
+
     for d in (1, 7, 2, 6, 3, 5, 4):
         us[d].wait_recv()
         at = (z - d + NZ) % NZ
         vs.append(send(ut.at[at], ut.at[NZ + at], v_send.at[d], v_recv.at[d], mate))
+
+    swap_y.wait_recv()
+    for i in range(NZ):
+        ys[i] = (ys[i].astype(F32) + r_y[i].astype(F32)).astype(BF16)
+    fwd = [
+        send(ys.at[(z + d) % NZ], r_fwd.at[d], y_send.at[d], y_recv.at[d], device((z + d) % NZ, yl, k, r))
+        for d in Z_ORDER
+    ]
 
     for copy in vs:
         copy.wait_recv()
@@ -274,36 +307,6 @@
             dev = device_xy(z, k, (x + d) % 4, y) if h == 0 else device_xy(z, k, x, (y + d) % 4)
             ones.append(send(bt.at[h, at], r_one.at[h, d], a_send.at[h, d], a_recv.at[h, d], dev))
 
-    for copy in xs:
-        copy.wait_recv()
-
-    def forward(i, carry):
-        rows = pl.ds(pl.multiple_of(OWN + i * 512, 512), 512)
-        total = jnp.dot(dense[0, rows, :], xall[0], preferred_element_type=F32)
-        total = total + jnp.dot(dense[1, rows, :], xall[1], preferred_element_type=F32)
-        ymate[pl.ds(4 * i, 4)] = total.astype(BF16).reshape(4, TILE, HID)
-        return carry
-
-    lax.fori_loop(0, 2, forward, 0)
-    swap_y = send(ymate, r_y, m_send, m_recv, mate)
-
-    def forward_own(i, carry):
-        rows = pl.ds(pl.multiple_of(i * 512, 512), 512)
-        total = jnp.dot(dense[0, rows, :], xall[0], preferred_element_type=F32)
-        total = total + jnp.dot(dense[1, rows, :], xall[1], preferred_element_type=F32)
-        ys[pl.ds(4 * i, 4)] = total.astype(BF16).reshape(4, TILE, HID)
-        return carry
-
-    lax.fori_loop(0, 2, forward_own, 0)
-
-    swap_y.wait_recv()
-    for i in range(NZ):
-        ys[i] = (ys[i].astype(F32) + r_y[i].astype(F32)).astype(BF16)
-    fwd = [
-        send(ys.at[(z + d) % NZ], r_fwd.at[d], y_send.at[d], y_recv.at[d], device((z + d) % NZ, yl, k, r))
-        for d in Z_ORDER
-    ]
-
     for copy in planes:
         copy.wait_recv()
     total = gs[spot]
@@ -384,7 +387,7 @@
     vm = pltpu.VMEM
     i32 = jnp.int32
     scratch = [
-        vm((4, 40, TILE), i32), vm((4, 40, TILE), i32), vm((8, 4, 8, TILE), i32), vm((32, 8, TILE), i32), vm((32, TILE), i32), pltpu.SMEM((32, TILE), i32),
+        vm((F_IN, OWN), BF16), vm((4, 40, TILE), i32), vm((4, 40, TILE), i32), vm((8, 4, 8, TILE), i32), vm((32, 8, TILE), i32), vm((32, TILE), i32), pltpu.SMEM((32, TILE), i32),
         vm((32, 5, TILE, TILE), BF16), vm((2, 2 * OWN, OWN), BF16), vm((2, OWN, HID), BF16),
         vm((F_IN, OWN), BF16), vm((8, TILE), i32), vm((2 * NZ, HID, TILE), BF16),
         vm((HID, 2 * OWN), BF16), vm((2, HID, OWN), BF16),
@@ -393,7 +396,7 @@
         vm((2, 4, TILE, TILE), BF16), vm((2, 4, TILE, TILE), BF16),
         vm((2, F_PAD, TILE), F32), vm((F_PAD, TILE), F32), vm((16, CHUNK, TILE), F32), vm((16, CHUNK, TILE), F32),
         vm((NZ, CHUNK, TILE), F32),
-        dma, dma((4,)), dma((4,)), dma((8,)), dma((8,)), dma((4,)), dma((4,)),
+        dma, dma, dma((4,)), dma((4,)), dma((8,)), dma((8,)), dma((4,)), dma((4,)),
         dma((8,)), dma((8,)), dma((8,)), dma((8,)), dma((2,)), dma((2,)), dma((4,)), dma((4,)),
         dma, dma, dma((8,)), dma((8,)), dma((2, 4)), dma((2, 4)), dma((2, 4)), dma((2, 4)),
         dma, dma, dma((16,)), dma((16,)), dma((8,)), dma((8,)), dma((16,)), dma((16,)), dma, dma,
@@ -405,7 +408,7 @@
             jax.ShapeDtypeStruct((F_IN, TILE), BF16),
             jax.ShapeDtypeStruct((16, CHUNK, HID), F32),
         ),
-        in_specs=[VM] * 6,
+        in_specs=[pl.BlockSpec(memory_space=pl.ANY)] + [VM] * 5,
         out_specs=(VM, VM, VM),
         scratch_shapes=scratch,
         compiler_params=pltpu.CompilerParams(

time: 81.1 us -> 68.3 us (0.84)
  Pallas kernels: 77 us -> 64.2 us
    pallas_call x1, Pallas kernels: 77 us -> 64.2 us  [layer_call(): pl.pallas_call(functools.partial(layer_kernel, scale), out_shape=(jax.Sha...]
where the time goes in v4:
time: 68.3 us; the launch traced here: 68.2 us
  Pallas kernels  64.2 us (94%)
  local copies, waits for them, and re-layouts  3.28 us (5%)
    pallas_call x1, Pallas kernels, layer_call(): pl.pallas_call(functools.partial(layer_kernel, scale), out_shape=(jax.Sha...  64.2 us
    slice x1, local copies, waits for them, and re-layouts, per_device(): return (out, gw.reshape(F_PAD, HID)[:F_IN], gin.T)  1.98 us

profile of v4, /device:TPU:1, one launch (start us, length us, event | category | flops | bytes accessed | tf_op | source)
XLA Modules:
  0.0 68.2 jit_solution(17950902510410915461)
XLA Ops:
  0.6 64.2 %shard_map.85 = (bf16[128,256]{1,0:T(8,128)(2,1)}, bf16[602,128]{1,0:T(8,128)(2,1)}, f32[16,40,256]{2,1,0:T(8,128)}) custom-call(bf16[602,1024]{1,0:T(8,128)(2,1)} %bitcast.6, bf16[602,256]{1,0:T(8,128)(2,1)} %weight.1, s32[8,128]{1,0:T(8,128)} %bitcast.10, bf16[128,256]{1,0:T(8,128)(2,1)} %cot.1, s32[4,32,128]{2,1,0:T(8,128)} %bitcast.9, s32[4,32]{1,0:T(4,128)} %bitcast.11), custom_call_target="tpu_custom_call" | custom-call | tf_op jit(solution)/shard_map/pallas_call | solution.py:404
  64.9 0.0 copy-start.1
  64.9 0.0 copy-start
  64.9 2.0 %slice.4 = f32[602,256]{1,0:T(8,128)} slice(f32[640,256]{1,0:T(8,128)} %bitcast.7), slice={[0:602], [0:256]} | slice | bytes 1232896 | tf_op jit(solution)/shard_map/slice | solution.py:425
  66.9 0.0 copy-done.1
  66.9 0.6 copy.11
  67.5 0.0 copy-done
  67.5 0.7 copy.12
Async XLA Ops:
  64.9 2.0 %copy-start.1 = (bf16[128,256]{1,0:T(8,128)(2,1)S(1)}, bf16[128,256]{1,0:T(8,128)(2,1)}, u32[]{:S(2)}) copy-start(bf16[128,256]{1,0:T(8,128)(2,1)} %get-tuple-element.12) | copy-start | bytes 196612
  64.9 2.6 %copy-start = (bf16[602,128]{1,0:T(8,128)(2,1)S(1)}, bf16[602,128]{1,0:T(8,128)(2,1)}, u32[]{:S(2)}) copy-start(bf16[602,128]{1,0:T(8,128)(2,1)} %get-tuple-element.8) | copy-start | bytes 462340

commit v5 on v4

--- a/solution.py
+++ b/solution.py
@@ -15,6 +15,7 @@
 F_IN = 602
 F_PAD = 640
 CHUNK = F_PAD // 16
+WIRE = 48
 NZ = 8
 F32 = jnp.float32
 BF16 = jnp.bfloat16
@@ -46,7 +47,7 @@
 def layer_kernel(
     scale, feat_hbm, weight, deg, cot, codes, tiles,
     out, gin, gw,
-    feat, pairs, relay, chunks, got, spots, slots, tbuf, dense, xall, fother, dother, ut, utw, db,
+    gsend, feat, pairs, relay, chunks, got, spots, slots, tbuf, dense, xall, fother, dother, ut, utw, db,
     ymate, r_y, ys, r_fwd, bt, r_one, p_part, r_two, gp, r_swap, gs, r_plane, r_z,
     feat_sem, slot_sem, code_send, code_recv, c_send, c_recv, q_send, q_recv, u_send, u_recv, v_send, v_recv, x_send, x_recv, f_send, f_recv,
     m_send, m_recv, y_send, y_recv, a_send, a_recv, b_send, b_recv,
@@ -185,41 +186,43 @@
                 device_xy(z, k, (x + d) % 4, y),
             )
         )
-    for copy in cs:
-        copy.wait_recv()
-
-    spots[...] = got[:, 4, :]
-    slot_copy = pltpu.make_async_copy(spots, slots, slot_sem)
-    slot_copy.start()
-
     lanes = lax.broadcasted_iota(jnp.int32, (TILE, TILE), 0)
 
-    def build(i, carry):
-        block = got[i]
-        for m in range(4):
-            code = block[m : m + 1, :]
-            rows = jnp.where(lanes == (code >> 7), 1.0, 0.0).astype(BF16)
-            cols = jnp.where(lanes == (code & 127), 1.0, 0.0).astype(BF16)
-            counts = lax.dot_general(rows, cols, (((1,), (1,)), ((), ())), preferred_element_type=F32)
-            tbuf[i, m] = counts.astype(BF16)
-        tbuf[i, 4] = jnp.zeros((TILE, TILE), BF16)
+    def group(rs):
+        block = got[pl.ds(4 * rs, 4)]
+        where = block[:, 4, :]
+        spots[rs] = jnp.concatenate([where, where], axis=0)
+        slot_copy = pltpu.make_async_copy(spots.at[rs], slots.at[rs], slot_sem.at[rs])
+        slot_copy.start()
+        for i in range(4):
+            for m in range(4):
+                code = block[i, m : m + 1, :]
+                rows = jnp.where(lanes == (code >> 7), 1.0, 0.0).astype(BF16)
+                cols = jnp.where(lanes == (code & 127), 1.0, 0.0).astype(BF16)
+                counts = lax.dot_general(rows, cols, (((1,), (1,)), ((), ())), preferred_element_type=F32)
+                tbuf[i, m] = counts.astype(BF16)
+            tbuf[i, 4] = jnp.zeros((TILE, TILE), BF16)
+        slot_copy.wait()
+        for i in range(4):
+            zs, _, _ = code_source(i, rs)
+            w, c = (i // 2) * NZ + zs, i % 2
+            at_m = [slots[rs, i, 4 * r + m] % 8 for m in range(4)]
+            for j in range(8):
+                at = jnp.int32(4)
+                for m in range(4):
+                    at = jnp.where(at_m[m] == j, m, at)
+                dense[c, pl.ds(pl.multiple_of(w * TILE, TILE), TILE), j * TILE : (j + 1) * TILE] = tbuf[i, at]
+
+    group(r)
+
+    def arrived(n, carry):
+        d = jnp.where(n < 4, 2 * n, 2 * n - 7)
+        rs = (r - d + 8) % 8
+        remote(chunks.at[0], got.at[pl.ds(4 * rs, 4)], c_send.at[d], c_recv.at[d], mate).wait_recv()
+        group(rs)
         return carry
 
-    lax.fori_loop(0, 32, build, 0, unroll=8)
-    slot_copy.wait()
-
-    def fill(i, carry):
-        zs, _, _ = code_source(i % 4, i // 4)
-        w, c = ((i // 2) % 2) * NZ + zs, i % 2
-        at_m = [slots[i, 4 * r + m] % 8 for m in range(4)]
-        for j in range(8):
-            at = jnp.int32(4)
-            for m in range(4):
-                at = jnp.where(at_m[m] == j, m, at)
-            dense[c, pl.ds(pl.multiple_of(w * TILE, TILE), TILE), j * TILE : (j + 1) * TILE] = tbuf[i, at]
-        return carry
-
-    lax.fori_loop(0, 32, fill, 0)
+    lax.fori_loop(1, 8, arrived, 0)
 
     for copy in xs:
         copy.wait_recv()
@@ -291,12 +294,14 @@
     swap = send(gp.at[1 - k], r_swap, w_send, w_recv, mate)
     swap.wait_recv()
     gs[...] = (gp[k] + r_swap[...]).reshape(16, CHUNK, TILE)
+    gsend[:, 0:CHUNK, :] = gs[...].astype(BF16)
+    gsend[:, CHUNK:WIRE, :] = jnp.zeros((16, WIRE - CHUNK, TILE), BF16)
 
     planes = []
     for i in PLANE_ORDER:
         xd, yd = (x + i // 4) % 4, (y + i % 4) % 4
         planes.append(
-            send(gs.at[xd * 4 + yd], r_plane.at[i], g_send.at[i], g_recv.at[i], device_xy(z, k, xd, yd))
+            send(gsend.at[xd * 4 + yd], r_plane.at[i], g_send.at[i], g_recv.at[i], device_xy(z, k, xd, yd))
         )
 
     here = (x, y)
@@ -311,8 +316,8 @@
         copy.wait_recv()
     total = gs[spot]
     for i in range(1, 16):
-        total = total + r_plane[i]
-    r_z[z] = total
+        total = total + r_plane[i, 0:CHUNK, :].astype(F32)
+    r_z[z] = jnp.concatenate([total, jnp.zeros((WIRE - CHUNK, TILE), F32)], axis=0).astype(BF16)
     zs = [
         send(r_z.at[z], r_z.at[z], z_send.at[d], z_recv.at[d], device((z + d) % NZ, yl, k, r)) for d in Z_ORDER
     ]
@@ -337,9 +342,9 @@
 
     for copy in zs:
         copy.wait_recv()
-    total = r_z[0]
+    total = r_z[0, 0:CHUNK, :].astype(F32)
     for i in range(1, NZ):
-        total = total + r_z[i]
+        total = total + r_z[i, 0:CHUNK, :].astype(F32)
     half = pl.ds(pl.multiple_of(k * TILE, TILE), TILE)
     gw[spot, :, half] = total * scale
     spread = []
@@ -387,16 +392,16 @@
     vm = pltpu.VMEM
     i32 = jnp.int32
     scratch = [
-        vm((F_IN, OWN), BF16), vm((4, 40, TILE), i32), vm((4, 40, TILE), i32), vm((8, 4, 8, TILE), i32), vm((32, 8, TILE), i32), vm((32, TILE), i32), pltpu.SMEM((32, TILE), i32),
-        vm((32, 5, TILE, TILE), BF16), vm((2, 2 * OWN, OWN), BF16), vm((2, OWN, HID), BF16),
+        vm((16, WIRE, TILE), BF16), vm((F_IN, OWN), BF16), vm((4, 40, TILE), i32), vm((4, 40, TILE), i32), vm((8, 4, 8, TILE), i32), vm((32, 8, TILE), i32), vm((8, 8, TILE), i32), pltpu.SMEM((8, 8, TILE), i32),
+        vm((4, 5, TILE, TILE), BF16), vm((2, 2 * OWN, OWN), BF16), vm((2, OWN, HID), BF16),
         vm((F_IN, OWN), BF16), vm((8, TILE), i32), vm((2 * NZ, HID, TILE), BF16),
         vm((HID, 2 * OWN), BF16), vm((2, HID, OWN), BF16),
         vm((NZ, TILE, HID), BF16), vm((NZ, TILE, HID), BF16), vm((NZ, TILE, HID), BF16), vm((NZ, TILE, HID), BF16),
         vm((2, 4, 4, TILE, TILE), BF16), vm((2, 4, 4, TILE, TILE), BF16),
         vm((2, 4, TILE, TILE), BF16), vm((2, 4, TILE, TILE), BF16),
-        vm((2, F_PAD, TILE), F32), vm((F_PAD, TILE), F32), vm((16, CHUNK, TILE), F32), vm((16, CHUNK, TILE), F32),
-        vm((NZ, CHUNK, TILE), F32),
-        dma, dma, dma((4,)), dma((4,)), dma((8,)), dma((8,)), dma((4,)), dma((4,)),
+        vm((2, F_PAD, TILE), F32), vm((F_PAD, TILE), F32), vm((16, CHUNK, TILE), F32), vm((16, WIRE, TILE), BF16),
+        vm((NZ, WIRE, TILE), BF16),
+        dma, dma((8,)), dma((4,)), dma((4,)), dma((8,)), dma((8,)), dma((4,)), dma((4,)),
         dma((8,)), dma((8,)), dma((8,)), dma((8,)), dma((2,)), dma((2,)), dma((4,)), dma((4,)),
         dma, dma, dma((8,)), dma((8,)), dma((2, 4)), dma((2, 4)), dma((2, 4)), dma((2, 4)),
         dma, dma, dma((16,)), dma((16,)), dma((8,)), dma((8,)), dma((16,)), dma((16,)), dma, dma,

time: 68.3 us -> 67.7 us (level)
  no operation moved by 1% of the time
where the time goes in v5:
time: 67.7 us; the launch traced here: 67.5 us
  Pallas kernels  63.6 us (94%)
  local copies, waits for them, and re-layouts  3.28 us (5%)
    pallas_call x1, Pallas kernels, layer_call(): pl.pallas_call(functools.partial(layer_kernel, scale), out_shape=(jax.Sha...  63.6 us
    slice x1, local copies, waits for them, and re-layouts, per_device(): return (out, gw.reshape(F_PAD, HID)[:F_IN], gin.T)  1.98 us

profile of v5, /device:TPU:1, one launch (start us, length us, event | category | flops | bytes accessed | tf_op | source)
XLA Modules:
  0.0 67.5 jit_solution(3782872504686673642)
XLA Ops:
  0.6 63.6 %shard_map.85 = (bf16[128,256]{1,0:T(8,128)(2,1)}, bf16[602,128]{1,0:T(8,128)(2,1)}, f32[16,40,256]{2,1,0:T(8,128)}) custom-call(bf16[602,1024]{1,0:T(8,128)(2,1)} %bitcast.6, bf16[602,256]{1,0:T(8,128)(2,1)} %weight.1, s32[8,128]{1,0:T(8,128)} %bitcast.10, bf16[128,256]{1,0:T(8,128)(2,1)} %cot.1, s32[4,32,128]{2,1,0:T(8,128)} %bitcast.9, s32[4,32]{1,0:T(4,128)} %bitcast.11), custom_call_target="tpu_custom_call" | custom-call | tf_op jit(solution)/shard_map/pallas_call | solution.py:409
  64.2 0.0 copy-start.1
  64.2 0.0 copy-start
  64.2 2.0 %slice.4 = f32[602,256]{1,0:T(8,128)} slice(f32[640,256]{1,0:T(8,128)} %bitcast.7), slice={[0:602], [0:256]} | slice | bytes 1232896 | tf_op jit(solution)/shard_map/slice | solution.py:430
  66.2 0.0 copy-done.1
  66.2 0.6 copy.11
  66.9 0.0 copy-done
  66.9 0.7 copy.12
Async XLA Ops:
  64.2 2.0 %copy-start.1 = (bf16[128,256]{1,0:T(8,128)(2,1)S(1)}, bf16[128,256]{1,0:T(8,128)(2,1)}, u32[]{:S(2)}) copy-start(bf16[128,256]{1,0:T(8,128)(2,1)} %get-tuple-element.12) | copy-start | bytes 196612
  64.2 2.6 %copy-start = (bf16[602,128]{1,0:T(8,128)(2,1)S(1)}, bf16[602,128]{1,0:T(8,128)(2,1)}, u32[]{:S(2)}) copy-start(bf16[602,128]{1,0:T(8,128)(2,1)} %get-tuple-element.8) | copy-start | bytes 462340

commit v6 on v5

--- a/solution.py
+++ b/solution.py
@@ -371,9 +371,11 @@
     root_col = jnp.broadcast_to(own_root, (8, TILE)).T
     out[...] = (total * root_col[:, 0:1]).astype(BF16)
 
-    for copy in spread:
-        copy.wait_recv()
-    last = send(gw.at[:, :, half], gw.at[:, :, half], e_send, e_recv, mate)
+    last = [send(gw.at[spot, :, half], gw.at[spot, :, half], e_send.at[0], e_recv.at[0], mate)]
+    for i, copy in reversed(list(zip(PLANE_ORDER, spread))):
+        copy.wait_recv()
+        at = ((x - i // 4 + 4) % 4) * 4 + (y - i % 4 + 4) % 4
+        last.append(send(gw.at[at, :, half], gw.at[at, :, half], e_send.at[i], e_recv.at[i], mate))
 
     for j in range(4):
         _, mine, copy = code_copy(j)
@@ -382,7 +384,8 @@
         def _():
             copy.wait_send()
 
-    last.wait_recv()
+    for copy in last:
+        copy.wait_recv()
     for copy in pending:
         copy.wait_send()
 
@@ -404,7 +407,7 @@
         dma, dma((8,)), dma((4,)), dma((4,)), dma((8,)), dma((8,)), dma((4,)), dma((4,)),
         dma((8,)), dma((8,)), dma((8,)), dma((8,)), dma((2,)), dma((2,)), dma((4,)), dma((4,)),
         dma, dma, dma((8,)), dma((8,)), dma((2, 4)), dma((2, 4)), dma((2, 4)), dma((2, 4)),
-        dma, dma, dma((16,)), dma((16,)), dma((8,)), dma((8,)), dma((16,)), dma((16,)), dma, dma,
+        dma, dma, dma((16,)), dma((16,)), dma((8,)), dma((8,)), dma((16,)), dma((16,)), dma((16,)), dma((16,)),
     ]
     return pl.pallas_call(
         functools.partial(layer_kernel, scale),

time: 67.7 us -> 67.8 us (level)
  no operation moved by 1% of the time
where the time goes in v6:
time: 67.8 us; the launch traced here: 67.6 us
  Pallas kernels  63.7 us (94%)
  local copies, waits for them, and re-layouts  3.28 us (5%)
    pallas_call x1, Pallas kernels, layer_call(): pl.pallas_call(functools.partial(layer_kernel, scale), out_shape=(jax.Sha...  63.7 us
    slice x1, local copies, waits for them, and re-layouts, per_device(): return (out, gw.reshape(F_PAD, HID)[:F_IN], gin.T)  1.98 us

profile of v6, /device:TPU:1, one launch (start us, length us, event | category | flops | bytes accessed | tf_op | source)
XLA Modules:
  0.0 67.6 jit_solution(10749201167724884949)
XLA Ops:
  0.6 63.7 %shard_map.85 = (bf16[128,256]{1,0:T(8,128)(2,1)}, bf16[602,128]{1,0:T(8,128)(2,1)}, f32[16,40,256]{2,1,0:T(8,128)}) custom-call(bf16[602,1024]{1,0:T(8,128)(2,1)} %bitcast.6, bf16[602,256]{1,0:T(8,128)(2,1)} %weight.1, s32[8,128]{1,0:T(8,128)} %bitcast.10, bf16[128,256]{1,0:T(8,128)(2,1)} %cot.1, s32[4,32,128]{2,1,0:T(8,128)} %bitcast.9, s32[4,32]{1,0:T(4,128)} %bitcast.11), custom_call_target="tpu_custom_call" | custom-call | tf_op jit(solution)/shard_map/pallas_call | solution.py:412
  64.3 0.0 copy-start.1
  64.3 0.0 copy-start
  64.3 2.0 %slice.4 = f32[602,256]{1,0:T(8,128)} slice(f32[640,256]{1,0:T(8,128)} %bitcast.7), slice={[0:602], [0:256]} | slice | bytes 1232896 | tf_op jit(solution)/shard_map/slice | solution.py:433
  66.3 0.0 copy-done.1
  66.3 0.6 copy.11
  67.0 0.0 copy-done
  67.0 0.7 copy.12
Async XLA Ops:
  64.3 2.0 %copy-start.1 = (bf16[128,256]{1,0:T(8,128)(2,1)S(1)}, bf16[128,256]{1,0:T(8,128)(2,1)}, u32[]{:S(2)}) copy-start(bf16[128,256]{1,0:T(8,128)(2,1)} %get-tuple-element.12) | copy-start | bytes 196612
  64.3 2.6 %copy-start = (bf16[602,128]{1,0:T(8,128)(2,1)S(1)}, bf16[602,128]{1,0:T(8,128)(2,1)}, u32[]{:S(2)}) copy-start(bf16[602,128]{1,0:T(8,128)(2,1)} %get-tuple-element.8) | copy-start | bytes 462340
